TPU v7x, 256 devices: a whole 4x4x8 slice. The times are simulated.
256 devices in a mesh: tm: 8 (over z), space: 32 (over x, y, core).
Axes of the slice: x: 4, y: 4, z: 8, core: 2. Of those that a mesh axis runs over, the one named last changes fastest.
Arguments:
- c_points: float32 [8, 160, 96, 256], P('tm', 'space'), may hold values from -6 to 6
- region: int32 [160, 96, 256], P('space'), may hold values from 0 to 2
- cond_scale: float32 [160, 96, 256], P('space'), may hold values from 0.5 to 2
- source: float32 [160, 96, 256], P('space'), may hold values from -6 to 6
- plan: int32 [32], P('tm'), may hold values from 0 to 3
Outputs:
- fine_states: float32 [32, 160, 96, 256], P('tm', 'space')
- corrected: float32 [8, 160, 96, 256], P('tm', 'space')
All inputs are finite; a program needn't handle non-finite values.
Results may differ from a plain program's by a relative error of at most 0.00002.
Values sent between devices are 32-bit elements; how exact they have to be, the bound alone decides.
No kernel may reach another device: no remote copies, remote signals or barrier semaphores. Data moves between devices by JAX's collectives and lax.ppermute only.
A program may use at most 128 MiB of HBM per device.

v0:
```python
import jax
import jax.numpy as jnp
from jax import lax
from jax.sharding import PartitionSpec as P

COARSEN = 4
SWEEPS = 4


FINE_RATE = 4.0


def with_halo(block, sides, width):
    for axis, dim in sides:
        count = lax.axis_size(axis)
        forward = [(i, i + 1) for i in range(count - 1)]
        backward = [(target, source) for source, target in forward]
        low = lax.ppermute(
            lax.slice_in_dim(block, block.shape[dim] - width, None, axis=dim), axis, forward
        )
        high = lax.ppermute(lax.slice_in_dim(block, 0, width, axis=dim), axis, backward)
        block = jnp.concatenate([low, block, high], axis=dim)
    return block


def shifted(shard, axis, by):
    size = lax.axis_size(axis)
    pairs = [(i, i + by) for i in range(size) if 0 <= i + by < size]
    return lax.ppermute(shard, axis, pairs)


def materials(region, cond_scale):
    cap = jnp.where(region == 0, 2.0, jnp.where(region == 1, 1.2, 1.6)).astype(jnp.float32)
    base = jnp.where(region == 0, 0.3, jnp.where(region == 1, 4.0, 2.5)).astype(jnp.float32)
    return (cap, base * cond_scale)


def side_pad(field):
    return jnp.pad(field, ((0, 0), (1, 1), (1, 1)))


def faces_from(cond_rim):
    padded = side_pad(cond_rim)
    center = padded[1:-1, 1:-1, 1:-1]
    return (
        0.5 * (center + padded[:-2, 1:-1, 1:-1]),
        0.5 * (center + padded[2:, 1:-1, 1:-1]),
        0.5 * (center + padded[1:-1, :-2, 1:-1]),
        0.5 * (center + padded[1:-1, 2:, 1:-1]),
        0.5 * (center + padded[1:-1, 1:-1, :-2]),
        0.5 * (center + padded[1:-1, 1:-1, 2:]),
    )


def sweep_sum(rhs, faces, up):
    f0, f1, f2, f3, f4, f5 = faces
    total = rhs + f0 * up[:-2, 1:-1, 1:-1] + f1 * up[2:, 1:-1, 1:-1]
    total = total + f2 * up[1:-1, :-2, 1:-1] + f3 * up[1:-1, 2:, 1:-1]
    total = total + f4 * up[1:-1, 1:-1, :-2] + f5 * up[1:-1, 1:-1, 2:]
    return total


def face_total(faces):
    f0, f1, f2, f3, f4, f5 = faces
    return f0 + f1 + f2 + f3 + f4 + f5


def on_device(c_points, region, cond_scale, source, plan):
    cap, cond = materials(region, cond_scale)
    cond_rim = with_halo(cond, (("space", 0),), 1)
    faces = faces_from(cond_rim)
    summed = face_total(faces)

    def implicit(u_old, amp, rate):
        diag = cap * rate + summed
        rhs = cap * rate * u_old + amp * source
        field = u_old
        for sweep in range(SWEEPS):
            up = with_halo(field, (("space", 0),), 1)
            field = sweep_sum(rhs, faces, side_pad(up)) / diag
        return field

    local_coarse = c_points.shape[0]
    amps = plan.astype(jnp.float32) * 0.5
    amp_mean = jnp.mean(amps.reshape(local_coarse, COARSEN), axis=1)
    coarse_rate = FINE_RATE / COARSEN
    fine = []
    field = c_points[0]
    for j in range(COARSEN):
        field = implicit(field, amps[j], FINE_RATE)
        fine.append(field)
    tau = [field - implicit(c_points[0], amp_mean[0], coarse_rate)]
    tau_all = jnp.stack(tau)
    groups = lax.axis_size("tm")
    group_index = lax.axis_index("tm")
    first_group = group_index == 0

    def one_round(turn, carried):
        incoming = shifted(carried[-1], "tm", 1)
        state = jnp.where(first_group, c_points[0], incoming)
        state = implicit(state, amp_mean[0], coarse_rate) + tau_all[0]
        result = [state]
        return jnp.stack(result)

    start = jnp.zeros(c_points.shape, jnp.float32)
    corrected = lax.fori_loop(0, groups, one_round, start)
    return (jnp.stack(fine), corrected)


def solution(mesh):
    in_specs = (
        P("tm", "space", None, None),
        P("space", None, None),
        P("space", None, None),
        P("space", None, None),
        P("tm"),
    )
    out_specs = (P("tm", "space", None, None), P("tm", "space", None, None))
    return jax.shard_map(
        on_device, mesh=mesh, in_specs=in_specs, out_specs=out_specs, check_vma=False
    )
```

profile of v0, /device:TPU:134, one launch (start us, length us, event | category | flops | bytes accessed | tf_op | source)
XLA Modules:
  0.0 724.2 jit_solution(9599080830428235923)
XLA Ops:
  2.8 4.8 collective-permute-start.11
  11.5 5.8 collective-permute-start.12
  20.9 3.0 add_divide_fusion
  27.2 5.8 collective-permute-start.14
  38.2 5.8 collective-permute-start.16
  49.3 5.8 collective-permute-start.18
  60.5 5.8 collective-permute-start.20
  72.3 5.8 collective-permute-start.22
  84.0 5.8 collective-permute-start.24
  97.2 6.0 collective-permute-start.26
  111.4 5.8 collective-permute-start.28
  119.2 5.8 collective-permute-start.44
  128.6 5.8 collective-permute-start.30
  140.3 5.8 collective-permute-start.32
  152.0 5.8 collective-permute-start.34
  159.9 5.8 collective-permute-start.46
  169.3 5.8 collective-permute-start.36
  181.0 5.8 collective-permute-start.38
  192.9 5.8 collective-permute-start.40
  200.7 6.0 collective-permute-start.48
  210.5 5.8 collective-permute-start.42
  223.8 500.3 %while.12 = (s32[]{:T(128)}, f32[1,5,96,256]{3,2,1,0:T(8,128)}, pred[]{:T(512)}, f32[1,5,96,256]{3,2,1,0:T(8,128)}, f32[5,96,256]{2,1,0:T(8,128)}, /*index=5*/f3...) while((s32[]{:T(128)}, f32[1,5,96,256]{3,2,1,0:T(8,128)}, ...), condition=%wide.region_2.3_spmd, body=%wide.region_1.2_spmd.sunk | while | flops 18606480 | bytes 57292932 | solution.py:106
  223.8 2.9 collective-permute-start
  226.8 9.2 %collective-permute-done = f32[5,96,256]{2,1,0:T(8,128)S(1)} collective-permute-done((f32[5,96,256]{2,1,0:T(8,128)}, f32[5,96,256]{2,1,0:T(8,128)S(1)}, u32[]{:S(2)}, u32[]{:S(2)}) %collective-permute-start) | collective-permute-done | bytes 491552 | tf_op jit(solution)/shard_map/while/body/eval_jaxpr/ppermute | solution.py:29
  237.1 5.7 collective-permute-start.1
  245.0 5.9 collective-permute-done.2
  256.3 5.6 collective-permute-done.4
  267.3 5.6 collective-permute-done.6
  279.8 5.9 collective-permute-done.8
  291.2 10.5 %collective-permute-done = f32[5,96,256]{2,1,0:T(8,128)S(1)} collective-permute-done((f32[5,96,256]{2,1,0:T(8,128)}, f32[5,96,256]{2,1,0:T(8,128)S(1)}, u32[]{:S(2)}, u32[]{:S(2)}) %collective-permute-start) | collective-permute-done | bytes 491552 | tf_op jit(solution)/shard_map/while/body/eval_jaxpr/ppermute | solution.py:29
  307.4 5.6 collective-permute-done.2
  318.4 5.6 collective-permute-done.4
  329.4 5.6 collective-permute-done.6
  341.9 5.9 collective-permute-done.8
  353.4 10.5 %collective-permute-done = f32[5,96,256]{2,1,0:T(8,128)S(1)} collective-permute-done((f32[5,96,256]{2,1,0:T(8,128)}, f32[5,96,256]{2,1,0:T(8,128)S(1)}, u32[]{:S(2)}, u32[]{:S(2)}) %collective-permute-start) | collective-permute-done | bytes 491552 | tf_op jit(solution)/shard_map/while/body/eval_jaxpr/ppermute | solution.py:29
  369.5 5.6 collective-permute-done.2
  380.6 5.6 collective-permute-done.4
  391.5 5.6 collective-permute-done.6
  404.0 5.9 collective-permute-done.8
  415.5 10.5 %collective-permute-done = f32[5,96,256]{2,1,0:T(8,128)S(1)} collective-permute-done((f32[5,96,256]{2,1,0:T(8,128)}, f32[5,96,256]{2,1,0:T(8,128)S(1)}, u32[]{:S(2)}, u32[]{:S(2)}) %collective-permute-start) | collective-permute-done | bytes 491552 | tf_op jit(solution)/shard_map/while/body/eval_jaxpr/ppermute | solution.py:29
  431.6 5.6 collective-permute-done.2
  442.7 5.6 collective-permute-done.4
  453.7 5.6 collective-permute-done.6
  466.2 5.9 collective-permute-done.8
  477.6 10.5 %collective-permute-done = f32[5,96,256]{2,1,0:T(8,128)S(1)} collective-permute-done((f32[5,96,256]{2,1,0:T(8,128)}, f32[5,96,256]{2,1,0:T(8,128)S(1)}, u32[]{:S(2)}, u32[]{:S(2)}) %collective-permute-start) | collective-permute-done | bytes 491552 | tf_op jit(solution)/shard_map/while/body/eval_jaxpr/ppermute | solution.py:29
  493.7 5.6 collective-permute-done.2
  504.8 5.6 collective-permute-done.4
  515.8 5.6 collective-permute-done.6
  528.3 5.9 collective-permute-done.8
  539.7 10.5 %collective-permute-done = f32[5,96,256]{2,1,0:T(8,128)S(1)} collective-permute-done((f32[5,96,256]{2,1,0:T(8,128)}, f32[5,96,256]{2,1,0:T(8,128)S(1)}, u32[]{:S(2)}, u32[]{:S(2)}) %collective-permute-start) | collective-permute-done | bytes 491552 | tf_op jit(solution)/shard_map/while/body/eval_jaxpr/ppermute | solution.py:29
  555.9 5.6 collective-permute-done.2
  566.9 5.6 collective-permute-done.4
  577.9 5.6 collective-permute-done.6
  590.4 5.9 collective-permute-done.8
  601.8 10.5 %collective-permute-done = f32[5,96,256]{2,1,0:T(8,128)S(1)} collective-permute-done((f32[5,96,256]{2,1,0:T(8,128)}, f32[5,96,256]{2,1,0:T(8,128)S(1)}, u32[]{:S(2)}, u32[]{:S(2)}) %collective-permute-start) | collective-permute-done | bytes 491552 | tf_op jit(solution)/shard_map/while/body/eval_jaxpr/ppermute | solution.py:29
  618.0 5.6 collective-permute-done.2
  629.0 5.6 collective-permute-done.4
  640.0 5.6 collective-permute-done.6
  652.5 5.9 collective-permute-done.8
  664.0 10.5 %collective-permute-done = f32[5,96,256]{2,1,0:T(8,128)S(1)} collective-permute-done((f32[5,96,256]{2,1,0:T(8,128)}, f32[5,96,256]{2,1,0:T(8,128)S(1)}, u32[]{:S(2)}, u32[]{:S(2)}) %collective-permute-start) | collective-permute-done | bytes 491552 | tf_op jit(solution)/shard_map/while/body/eval_jaxpr/ppermute | solution.py:29
  680.1 5.6 collective-permute-done.2
  691.2 5.6 collective-permute-done.4
  702.1 5.6 collective-permute-done.6
  714.6 5.9 collective-permute-done.8
  (484 shorter events, 327.9 us)
Async XLA Ops:
  2.8 16.4 %collective-permute-start.11 = (f32[1,96,256]{2,1,0:T(8,128)S(1)}, f32[1,96,256]{2,1,0:T(8,128)S(1)}, u32[]{:S(2)}, u32[]{:S(2)}) collective-permute-start(f32[1,96,256]{2,1,0:T(8,128)S(1)} %get-tuple-element.285), channel_id=1, source_target_pairs={{1,0},{2,1},{3,2},{4,3},{5,4},{6,5},{7,6},{8,7},{9,8},{10,9},{11,1... | collective-permute-start | bytes 294920 | tf_op jit(solution)/shard_map/ppermute | solution.py:21
  7.6 11.6 %collective-permute-start.9 = (f32[1,96,256]{2,1,0:T(8,128)S(1)}, f32[1,96,256]{2,1,0:T(8,128)S(1)}, u32[]{:S(2)}, u32[]{:S(2)}) collective-permute-start(f32[1,96,256]{2,1,0:T(8,128)S(1)} %get-tuple-element.284), channel_id=1, source_target_pairs={{0,1},{1,2},{2,3},{3,4},{4,5},{5,6},{6,7},{7,8},{8,9},{9,10},{10,1... | collective-permute-start | bytes 294920 | tf_op jit(solution)/shard_map/ppermute | solution.py:18
  9.6 10.1 %collective-permute-start.10 = (f32[1,96,256]{2,1,0:T(8,128)S(1)}, f32[1,96,256]{2,1,0:T(8,128)S(1)}, u32[]{:S(2)}, u32[]{:S(2)}) collective-permute-start(f32[1,96,256]{2,1,0:T(8,128)S(1)} %get-tuple-element.286), channel_id=1, source_target_pairs={{0,1},{1,2},{2,3},{3,4},{4,5},{5,6},{6,7},{7,8},{8,9},{9,10},{10,1... | collective-permute-start | bytes 294920 | tf_op jit(solution)/shard_map/ppermute | solution.py:18
  11.5 8.2 %collective-permute-start.12 = (f32[1,96,256]{2,1,0:T(8,128)S(1)}, f32[1,96,256]{2,1,0:T(8,128)S(1)}, u32[]{:S(2)}, u32[]{:S(2)}) collective-permute-start(f32[1,96,256]{2,1,0:T(8,128)S(1)} %get-tuple-element.287), channel_id=1, source_target_pairs={{1,0},{2,1},{3,2},{4,3},{5,4},{6,5},{7,6},{8,7},{9,8},{10,9},{11,1... | collective-permute-start | bytes 294920 | tf_op jit(solution)/shard_map/ppermute | solution.py:21
  25.3 8.0 %collective-permute-start.13 = (f32[1,96,256]{2,1,0:T(8,128)S(1)}, f32[1,96,256]{2,1,0:T(8,128)S(1)}, u32[]{:S(2)}, u32[]{:S(2)}) collective-permute-start(f32[1,96,256]{2,1,0:T(8,128)S(1)} %get-tuple-element.276), channel_id=1, source_target_pairs={{0,1},{1,2},{2,3},{3,4},{4,5},{5,6},{6,7},{7,8},{8,9},{9,10},{10,1... | collective-permute-start | bytes 294920 | tf_op jit(solution)/shard_map/ppermute | solution.py:18
  36.3 8.1 %collective-permute-start.15 = (f32[1,96,256]{2,1,0:T(8,128)S(1)}, f32[1,96,256]{2,1,0:T(8,128)S(1)}, u32[]{:S(2)}, u32[]{:S(2)}) collective-permute-start(f32[1,96,256]{2,1,0:T(8,128)S(1)} %get-tuple-element.274), channel_id=1, source_target_pairs={{0,1},{1,2},{2,3},{3,4},{4,5},{5,6},{6,7},{7,8},{8,9},{9,10},{10,1... | collective-permute-start | bytes 294920 | tf_op jit(solution)/shard_map/ppermute | solution.py:18
  38.2 8.0 %collective-permute-start.16 = (f32[1,96,256]{2,1,0:T(8,128)S(1)}, f32[1,96,256]{2,1,0:T(8,128)S(1)}, u32[]{:S(2)}, u32[]{:S(2)}) collective-permute-start(f32[1,96,256]{2,1,0:T(8,128)S(1)} %get-tuple-element.275), channel_id=1, source_target_pairs={{1,0},{2,1},{3,2},{4,3},{5,4},{6,5},{7,6},{8,7},{9,8},{10,9},{11,1... | collective-permute-start | bytes 294920 | tf_op jit(solution)/shard_map/ppermute | solution.py:21
  47.3 8.1 %collective-permute-start.17 = (f32[1,96,256]{2,1,0:T(8,128)S(1)}, f32[1,96,256]{2,1,0:T(8,128)S(1)}, u32[]{:S(2)}, u32[]{:S(2)}) collective-permute-start(f32[1,96,256]{2,1,0:T(8,128)S(1)} %get-tuple-element.272), channel_id=1, source_target_pairs={{0,1},{1,2},{2,3},{3,4},{4,5},{5,6},{6,7},{7,8},{8,9},{9,10},{10,1... | collective-permute-start | bytes 294920 | tf_op jit(solution)/shard_map/ppermute | solution.py:18
  49.3 8.0 %collective-permute-start.18 = (f32[1,96,256]{2,1,0:T(8,128)S(1)}, f32[1,96,256]{2,1,0:T(8,128)S(1)}, u32[]{:S(2)}, u32[]{:S(2)}) collective-permute-start(f32[1,96,256]{2,1,0:T(8,128)S(1)} %get-tuple-element.273), channel_id=1, source_target_pairs={{1,0},{2,1},{3,2},{4,3},{5,4},{6,5},{7,6},{8,7},{9,8},{10,9},{11,1... | collective-permute-start | bytes 294920 | tf_op jit(solution)/shard_map/ppermute | solution.py:21
  58.4 8.3 %collective-permute-start.19 = (f32[1,96,256]{2,1,0:T(8,128)S(1)}, f32[1,96,256]{2,1,0:T(8,128)S(1)}, u32[]{:S(2)}, u32[]{:S(2)}) collective-permute-start(f32[1,96,256]{2,1,0:T(8,128)S(1)} %get-tuple-element.270), channel_id=1, source_target_pairs={{0,1},{1,2},{2,3},{3,4},{4,5},{5,6},{6,7},{7,8},{8,9},{9,10},{10,1... | collective-permute-start | bytes 294920 | tf_op jit(solution)/shard_map/ppermute | solution.py:18
  60.5 8.0 %collective-permute-start.20 = (f32[1,96,256]{2,1,0:T(8,128)S(1)}, f32[1,96,256]{2,1,0:T(8,128)S(1)}, u32[]{:S(2)}, u32[]{:S(2)}) collective-permute-start(f32[1,96,256]{2,1,0:T(8,128)S(1)} %get-tuple-element.271), channel_id=1, source_target_pairs={{1,0},{2,1},{3,2},{4,3},{5,4},{6,5},{7,6},{8,7},{9,8},{10,9},{11,1... | collective-permute-start | bytes 294920 | tf_op jit(solution)/shard_map/ppermute | solution.py:21
  70.3 8.1 %collective-permute-start.21 = (f32[1,96,256]{2,1,0:T(8,128)S(1)}, f32[1,96,256]{2,1,0:T(8,128)S(1)}, u32[]{:S(2)}, u32[]{:S(2)}) collective-permute-start(f32[1,96,256]{2,1,0:T(8,128)S(1)} %get-tuple-element.268), channel_id=1, source_target_pairs={{0,1},{1,2},{2,3},{3,4},{4,5},{5,6},{6,7},{7,8},{8,9},{9,10},{10,1... | collective-permute-start | bytes 294920 | tf_op jit(solution)/shard_map/ppermute | solution.py:18
  72.3 8.0 %collective-permute-start.22 = (f32[1,96,256]{2,1,0:T(8,128)S(1)}, f32[1,96,256]{2,1,0:T(8,128)S(1)}, u32[]{:S(2)}, u32[]{:S(2)}) collective-permute-start(f32[1,96,256]{2,1,0:T(8,128)S(1)} %get-tuple-element.269), channel_id=1, source_target_pairs={{1,0},{2,1},{3,2},{4,3},{5,4},{6,5},{7,6},{8,7},{9,8},{10,9},{11,1... | collective-permute-start | bytes 294920 | tf_op jit(solution)/shard_map/ppermute | solution.py:21
  82.1 8.1 %collective-permute-start.23 = (f32[1,96,256]{2,1,0:T(8,128)S(1)}, f32[1,96,256]{2,1,0:T(8,128)S(1)}, u32[]{:S(2)}, u32[]{:S(2)}) collective-permute-start(f32[1,96,256]{2,1,0:T(8,128)S(1)} %get-tuple-element.266), channel_id=1, source_target_pairs={{0,1},{1,2},{2,3},{3,4},{4,5},{5,6},{6,7},{7,8},{8,9},{9,10},{10,1... | collective-permute-start | bytes 294920 | tf_op jit(solution)/shard_map/ppermute | solution.py:18
  84.0 8.0 %collective-permute-start.24 = (f32[1,96,256]{2,1,0:T(8,128)S(1)}, f32[1,96,256]{2,1,0:T(8,128)S(1)}, u32[]{:S(2)}, u32[]{:S(2)}) collective-permute-start(f32[1,96,256]{2,1,0:T(8,128)S(1)} %get-tuple-element.267), channel_id=1, source_target_pairs={{1,0},{2,1},{3,2},{4,3},{5,4},{6,5},{7,6},{8,7},{9,8},{10,9},{11,1... | collective-permute-start | bytes 294920 | tf_op jit(solution)/shard_map/ppermute | solution.py:21
  95.3 8.3 %collective-permute-start.25 = (f32[1,96,256]{2,1,0:T(8,128)}, f32[1,96,256]{2,1,0:T(8,128)S(1)}, u32[]{:S(2)}, u32[]{:S(2)}) collective-permute-start(f32[1,96,256]{2,1,0:T(8,128)} %get-tuple-element.264), channel_id=1, source_target_pairs={{0,1},{1,2},{2,3},{3,4},{4,5},{5,6},{6,7},{7,8},{8,9},{9,10},{10,1... | collective-permute-start | bytes 294920 | tf_op jit(solution)/shard_map/ppermute | solution.py:18
  97.2 8.4 %collective-permute-start.26 = (f32[1,96,256]{2,1,0:T(8,128)}, f32[1,96,256]{2,1,0:T(8,128)}, u32[]{:S(2)}, u32[]{:S(2)}) collective-permute-start(f32[1,96,256]{2,1,0:T(8,128)} %get-tuple-element.265), channel_id=1, source_target_pairs={{1,0},{2,1},{3,2},{4,3},{5,4},{6,5},{7,6},{8,7},{9,8},{10,9},{11,1... | collective-permute-start | bytes 294920 | tf_op jit(solution)/shard_map/ppermute | solution.py:21
  109.4 15.5 %collective-permute-start.27 = (f32[1,96,256]{2,1,0:T(8,128)S(1)}, f32[1,96,256]{2,1,0:T(8,128)S(1)}, u32[]{:S(2)}, u32[]{:S(2)}) collective-permute-start(f32[1,96,256]{2,1,0:T(8,128)S(1)} %get-tuple-element.262), channel_id=1, source_target_pairs={{0,1},{1,2},{2,3},{3,4},{4,5},{5,6},{6,7},{7,8},{8,9},{9,10},{10,1... | collective-permute-start | bytes 294920 | tf_op jit(solution)/shard_map/ppermute | solution.py:18
  111.4 13.6 %collective-permute-start.28 = (f32[1,96,256]{2,1,0:T(8,128)S(1)}, f32[1,96,256]{2,1,0:T(8,128)S(1)}, u32[]{:S(2)}, u32[]{:S(2)}) collective-permute-start(f32[1,96,256]{2,1,0:T(8,128)S(1)} %get-tuple-element.263), channel_id=1, source_target_pairs={{1,0},{2,1},{3,2},{4,3},{5,4},{6,5},{7,6},{8,7},{9,8},{10,9},{11,1... | collective-permute-start | bytes 294920 | tf_op jit(solution)/shard_map/ppermute | solution.py:21
  117.3 17.1 %collective-permute-start.43 = (f32[1,96,256]{2,1,0:T(8,128)S(1)}, f32[1,96,256]{2,1,0:T(8,128)S(1)}, u32[]{:S(2)}, u32[]{:S(2)}) collective-permute-start(f32[1,96,256]{2,1,0:T(8,128)S(1)} %get-tuple-element.282), channel_id=1, source_target_pairs={{0,1},{1,2},{2,3},{3,4},{4,5},{5,6},{6,7},{7,8},{8,9},{9,10},{10,1... | collective-permute-start | bytes 294920 | tf_op jit(solution)/shard_map/ppermute | solution.py:18
  119.2 15.2 %collective-permute-start.44 = (f32[1,96,256]{2,1,0:T(8,128)S(1)}, f32[1,96,256]{2,1,0:T(8,128)S(1)}, u32[]{:S(2)}, u32[]{:S(2)}) collective-permute-start(f32[1,96,256]{2,1,0:T(8,128)S(1)} %get-tuple-element.283), channel_id=1, source_target_pairs={{1,0},{2,1},{3,2},{4,3},{5,4},{6,5},{7,6},{8,7},{9,8},{10,9},{11,1... | collective-permute-start | bytes 294920 | tf_op jit(solution)/shard_map/ppermute | solution.py:21
  126.7 8.1 %collective-permute-start.29 = (f32[1,96,256]{2,1,0:T(8,128)S(1)}, f32[1,96,256]{2,1,0:T(8,128)S(1)}, u32[]{:S(2)}, u32[]{:S(2)}) collective-permute-start(f32[1,96,256]{2,1,0:T(8,128)S(1)} %get-tuple-element.260), channel_id=1, source_target_pairs={{0,1},{1,2},{2,3},{3,4},{4,5},{5,6},{6,7},{7,8},{8,9},{9,10},{10,1... | collective-permute-start | bytes 294920 | tf_op jit(solution)/shard_map/ppermute | solution.py:18
  138.4 8.5 %collective-permute-start.31 = (f32[1,96,256]{2,1,0:T(8,128)S(1)}, f32[1,96,256]{2,1,0:T(8,128)S(1)}, u32[]{:S(2)}, u32[]{:S(2)}) collective-permute-start(f32[1,96,256]{2,1,0:T(8,128)S(1)} %get-tuple-element.258), channel_id=1, source_target_pairs={{0,1},{1,2},{2,3},{3,4},{4,5},{5,6},{6,7},{7,8},{8,9},{9,10},{10,1... | collective-permute-start | bytes 294920 | tf_op jit(solution)/shard_map/ppermute | solution.py:18
  140.3 8.0 %collective-permute-start.32 = (f32[1,96,256]{2,1,0:T(8,128)S(1)}, f32[1,96,256]{2,1,0:T(8,128)S(1)}, u32[]{:S(2)}, u32[]{:S(2)}) collective-permute-start(f32[1,96,256]{2,1,0:T(8,128)S(1)} %get-tuple-element.259), channel_id=1, source_target_pairs={{1,0},{2,1},{3,2},{4,3},{5,4},{6,5},{7,6},{8,7},{9,8},{10,9},{11,1... | collective-permute-start | bytes 294920 | tf_op jit(solution)/shard_map/ppermute | solution.py:21
  150.1 15.5 %collective-permute-start.33 = (f32[1,96,256]{2,1,0:T(8,128)S(1)}, f32[1,96,256]{2,1,0:T(8,128)S(1)}, u32[]{:S(2)}, u32[]{:S(2)}) collective-permute-start(f32[1,96,256]{2,1,0:T(8,128)S(1)} %get-tuple-element.256), channel_id=1, source_target_pairs={{0,1},{1,2},{2,3},{3,4},{4,5},{5,6},{6,7},{7,8},{8,9},{9,10},{10,1... | collective-permute-start | bytes 294920 | tf_op jit(solution)/shard_map/ppermute | solution.py:18
  152.0 13.6 %collective-permute-start.34 = (f32[1,96,256]{2,1,0:T(8,128)S(1)}, f32[1,96,256]{2,1,0:T(8,128)S(1)}, u32[]{:S(2)}, u32[]{:S(2)}) collective-permute-start(f32[1,96,256]{2,1,0:T(8,128)S(1)} %get-tuple-element.257), channel_id=1, source_target_pairs={{1,0},{2,1},{3,2},{4,3},{5,4},{6,5},{7,6},{8,7},{9,8},{10,9},{11,1... | collective-permute-start | bytes 294920 | tf_op jit(solution)/shard_map/ppermute | solution.py:21
  157.9 17.1 %collective-permute-start.45 = (f32[1,96,256]{2,1,0:T(8,128)S(1)}, f32[1,96,256]{2,1,0:T(8,128)S(1)}, u32[]{:S(2)}, u32[]{:S(2)}) collective-permute-start(f32[1,96,256]{2,1,0:T(8,128)S(1)} %get-tuple-element.280), channel_id=1, source_target_pairs={{0,1},{1,2},{2,3},{3,4},{4,5},{5,6},{6,7},{7,8},{8,9},{9,10},{10,1... | collective-permute-start | bytes 294920 | tf_op jit(solution)/shard_map/ppermute | solution.py:18
  159.9 15.2 %collective-permute-start.46 = (f32[1,96,256]{2,1,0:T(8,128)S(1)}, f32[1,96,256]{2,1,0:T(8,128)S(1)}, u32[]{:S(2)}, u32[]{:S(2)}) collective-permute-start(f32[1,96,256]{2,1,0:T(8,128)S(1)} %get-tuple-element.281), channel_id=1, source_target_pairs={{1,0},{2,1},{3,2},{4,3},{5,4},{6,5},{7,6},{8,7},{9,8},{10,9},{11,1... | collective-permute-start | bytes 294920 | tf_op jit(solution)/shard_map/ppermute | solution.py:21
  167.4 8.1 %collective-permute-start.35 = (f32[1,96,256]{2,1,0:T(8,128)S(1)}, f32[1,96,256]{2,1,0:T(8,128)S(1)}, u32[]{:S(2)}, u32[]{:S(2)}) collective-permute-start(f32[1,96,256]{2,1,0:T(8,128)S(1)} %get-tuple-element.254), channel_id=1, source_target_pairs={{0,1},{1,2},{2,3},{3,4},{4,5},{5,6},{6,7},{7,8},{8,9},{9,10},{10,1... | collective-permute-start | bytes 294920 | tf_op jit(solution)/shard_map/ppermute | solution.py:18
  179.1 8.5 %collective-permute-start.37 = (f32[1,96,256]{2,1,0:T(8,128)S(1)}, f32[1,96,256]{2,1,0:T(8,128)S(1)}, u32[]{:S(2)}, u32[]{:S(2)}) collective-permute-start(f32[1,96,256]{2,1,0:T(8,128)S(1)} %get-tuple-element.252), channel_id=1, source_target_pairs={{0,1},{1,2},{2,3},{3,4},{4,5},{5,6},{6,7},{7,8},{8,9},{9,10},{10,1... | collective-permute-start | bytes 294920 | tf_op jit(solution)/shard_map/ppermute | solution.py:18
  181.0 8.0 %collective-permute-start.38 = (f32[1,96,256]{2,1,0:T(8,128)S(1)}, f32[1,96,256]{2,1,0:T(8,128)S(1)}, u32[]{:S(2)}, u32[]{:S(2)}) collective-permute-start(f32[1,96,256]{2,1,0:T(8,128)S(1)} %get-tuple-element.253), channel_id=1, source_target_pairs={{1,0},{2,1},{3,2},{4,3},{5,4},{6,5},{7,6},{8,7},{9,8},{10,9},{11,1... | collective-permute-start | bytes 294920 | tf_op jit(solution)/shard_map/ppermute | solution.py:21
  191.0 15.7 %collective-permute-start.39 = (f32[1,96,256]{2,1,0:T(8,128)S(1)}, f32[1,96,256]{2,1,0:T(8,128)S(1)}, u32[]{:S(2)}, u32[]{:S(2)}) collective-permute-start(f32[1,96,256]{2,1,0:T(8,128)S(1)} %get-tuple-element.250), channel_id=1, source_target_pairs={{0,1},{1,2},{2,3},{3,4},{4,5},{5,6},{6,7},{7,8},{8,9},{9,10},{10,1... | collective-permute-start | bytes 294920 | tf_op jit(solution)/shard_map/ppermute | solution.py:18
  192.9 13.8 %collective-permute-start.40 = (f32[1,96,256]{2,1,0:T(8,128)S(1)}, f32[1,96,256]{2,1,0:T(8,128)S(1)}, u32[]{:S(2)}, u32[]{:S(2)}) collective-permute-start(f32[1,96,256]{2,1,0:T(8,128)S(1)} %get-tuple-element.251), channel_id=1, source_target_pairs={{1,0},{2,1},{3,2},{4,3},{5,4},{6,5},{7,6},{8,7},{9,8},{10,9},{11,1... | collective-permute-start | bytes 294920 | tf_op jit(solution)/shard_map/ppermute | solution.py:21
  198.8 17.5 %collective-permute-start.47 = (f32[1,96,256]{2,1,0:T(8,128)S(1)}, f32[1,96,256]{2,1,0:T(8,128)S(1)}, u32[]{:S(2)}, u32[]{:S(2)}) collective-permute-start(f32[1,96,256]{2,1,0:T(8,128)S(1)} %get-tuple-element.278), channel_id=1, source_target_pairs={{0,1},{1,2},{2,3},{3,4},{4,5},{5,6},{6,7},{7,8},{8,9},{9,10},{10,1... | collective-permute-start | bytes 294920 | tf_op jit(solution)/shard_map/ppermute | solution.py:18
  200.7 15.6 %collective-permute-start.48 = (f32[1,96,256]{2,1,0:T(8,128)S(1)}, f32[1,96,256]{2,1,0:T(8,128)S(1)}, u32[]{:S(2)}, u32[]{:S(2)}) collective-permute-start(f32[1,96,256]{2,1,0:T(8,128)S(1)} %get-tuple-element.279), channel_id=1, source_target_pairs={{1,0},{2,1},{3,2},{4,3},{5,4},{6,5},{7,6},{8,7},{9,8},{10,9},{11,1... | collective-permute-start | bytes 294920 | tf_op jit(solution)/shard_map/ppermute | solution.py:21
  208.6 8.1 %collective-permute-start.41 = (f32[1,96,256]{2,1,0:T(8,128)S(1)}, f32[1,96,256]{2,1,0:T(8,128)S(1)}, u32[]{:S(2)}, u32[]{:S(2)}) collective-permute-start(f32[1,96,256]{2,1,0:T(8,128)S(1)} %get-tuple-element.248), channel_id=1, source_target_pairs={{0,1},{1,2},{2,3},{3,4},{4,5},{5,6},{6,7},{7,8},{8,9},{9,10},{10,1... | collective-permute-start | bytes 294920 | tf_op jit(solution)/shard_map/ppermute | solution.py:18
  223.8 12.1 %collective-permute-start = (f32[5,96,256]{2,1,0:T(8,128)}, f32[5,96,256]{2,1,0:T(8,128)S(1)}, u32[]{:S(2)}, u32[]{:S(2)}) collective-permute-start(f32[5,96,256]{2,1,0:T(8,128)} %bitcast.39), channel_id=1, source_target_pairs={{0,32},{32,64},{64,96},{96,128},{128,160},{160,192},{192,224},{1,3... | collective-permute-start | bytes 1474568 | tf_op jit(solution)/shard_map/while/body/eval_jaxpr/ppermute | solution.py:29
  242.8 8.0 %collective-permute-start.2 = (f32[1,96,256]{2,1,0:T(8,128)S(1)}, f32[1,96,256]{2,1,0:T(8,128)S(1)}, u32[]{:S(2)}, u32[]{:S(2)}) collective-permute-start(f32[1,96,256]{2,1,0:T(8,128)S(1)} %get-tuple-element.396), channel_id=1, source_target_pairs={{0,1},{1,2},{2,3},{3,4},{4,5},{5,6},{6,7},{7,8},{8,9},{9,10},{10,1... | collective-permute-start | bytes 294920 | tf_op jit(solution)/shard_map/while/body/eval_jaxpr/ppermute | solution.py:18
  253.9 8.0 %collective-permute-start.4 = (f32[1,96,256]{2,1,0:T(8,128)S(1)}, f32[1,96,256]{2,1,0:T(8,128)S(1)}, u32[]{:S(2)}, u32[]{:S(2)}) collective-permute-start(f32[1,96,256]{2,1,0:T(8,128)S(1)} %get-tuple-element.399), channel_id=1, source_target_pairs={{0,1},{1,2},{2,3},{3,4},{4,5},{5,6},{6,7},{7,8},{8,9},{9,10},{10,1... | collective-permute-start | bytes 294920 | tf_op jit(solution)/shard_map/while/body/eval_jaxpr/ppermute | solution.py:18
  264.9 8.0 %collective-permute-start.6 = (f32[1,96,256]{2,1,0:T(8,128)S(1)}, f32[1,96,256]{2,1,0:T(8,128)S(1)}, u32[]{:S(2)}, u32[]{:S(2)}) collective-permute-start(f32[1,96,256]{2,1,0:T(8,128)S(1)} %get-tuple-element.402), channel_id=1, source_target_pairs={{0,1},{1,2},{2,3},{3,4},{4,5},{5,6},{6,7},{7,8},{8,9},{9,10},{10,1... | collective-permute-start | bytes 294920 | tf_op jit(solution)/shard_map/while/body/eval_jaxpr/ppermute | solution.py:18
  277.3 8.4 %collective-permute-start.8 = (f32[1,96,256]{2,1,0:T(8,128)}, f32[1,96,256]{2,1,0:T(8,128)}, u32[]{:S(2)}, u32[]{:S(2)}) collective-permute-start(f32[1,96,256]{2,1,0:T(8,128)} %get-tuple-element.404), channel_id=1, source_target_pairs={{0,1},{1,2},{2,3},{3,4},{4,5},{5,6},{6,7},{7,8},{8,9},{9,10},{10,1... | collective-permute-start | bytes 294920 | tf_op jit(solution)/shard_map/while/body/eval_jaxpr/ppermute | solution.py:18
  289.3 12.4 %collective-permute-start = (f32[5,96,256]{2,1,0:T(8,128)}, f32[5,96,256]{2,1,0:T(8,128)S(1)}, u32[]{:S(2)}, u32[]{:S(2)}) collective-permute-start(f32[5,96,256]{2,1,0:T(8,128)} %bitcast.39), channel_id=1, source_target_pairs={{0,32},{32,64},{64,96},{96,128},{128,160},{160,192},{192,224},{1,3... | collective-permute-start | bytes 1474568 | tf_op jit(solution)/shard_map/while/body/eval_jaxpr/ppermute | solution.py:29
  305.0 8.0 %collective-permute-start.2 = (f32[1,96,256]{2,1,0:T(8,128)S(1)}, f32[1,96,256]{2,1,0:T(8,128)S(1)}, u32[]{:S(2)}, u32[]{:S(2)}) collective-permute-start(f32[1,96,256]{2,1,0:T(8,128)S(1)} %get-tuple-element.396), channel_id=1, source_target_pairs={{0,1},{1,2},{2,3},{3,4},{4,5},{5,6},{6,7},{7,8},{8,9},{9,10},{10,1... | collective-permute-start | bytes 294920 | tf_op jit(solution)/shard_map/while/body/eval_jaxpr/ppermute | solution.py:18
  316.0 8.0 %collective-permute-start.4 = (f32[1,96,256]{2,1,0:T(8,128)S(1)}, f32[1,96,256]{2,1,0:T(8,128)S(1)}, u32[]{:S(2)}, u32[]{:S(2)}) collective-permute-start(f32[1,96,256]{2,1,0:T(8,128)S(1)} %get-tuple-element.399), channel_id=1, source_target_pairs={{0,1},{1,2},{2,3},{3,4},{4,5},{5,6},{6,7},{7,8},{8,9},{9,10},{10,1... | collective-permute-start | bytes 294920 | tf_op jit(solution)/shard_map/while/body/eval_jaxpr/ppermute | solution.py:18
  327.0 8.0 %collective-permute-start.6 = (f32[1,96,256]{2,1,0:T(8,128)S(1)}, f32[1,96,256]{2,1,0:T(8,128)S(1)}, u32[]{:S(2)}, u32[]{:S(2)}) collective-permute-start(f32[1,96,256]{2,1,0:T(8,128)S(1)} %get-tuple-element.402), channel_id=1, source_target_pairs={{0,1},{1,2},{2,3},{3,4},{4,5},{5,6},{6,7},{7,8},{8,9},{9,10},{10,1... | collective-permute-start | bytes 294920 | tf_op jit(solution)/shard_map/while/body/eval_jaxpr/ppermute | solution.py:18
  339.4 8.4 %collective-permute-start.8 = (f32[1,96,256]{2,1,0:T(8,128)}, f32[1,96,256]{2,1,0:T(8,128)}, u32[]{:S(2)}, u32[]{:S(2)}) collective-permute-start(f32[1,96,256]{2,1,0:T(8,128)} %get-tuple-element.404), channel_id=1, source_target_pairs={{0,1},{1,2},{2,3},{3,4},{4,5},{5,6},{6,7},{7,8},{8,9},{9,10},{10,1... | collective-permute-start | bytes 294920 | tf_op jit(solution)/shard_map/while/body/eval_jaxpr/ppermute | solution.py:18
  351.4 12.4 %collective-permute-start = (f32[5,96,256]{2,1,0:T(8,128)}, f32[5,96,256]{2,1,0:T(8,128)S(1)}, u32[]{:S(2)}, u32[]{:S(2)}) collective-permute-start(f32[5,96,256]{2,1,0:T(8,128)} %bitcast.39), channel_id=1, source_target_pairs={{0,32},{32,64},{64,96},{96,128},{128,160},{160,192},{192,224},{1,3... | collective-permute-start | bytes 1474568 | tf_op jit(solution)/shard_map/while/body/eval_jaxpr/ppermute | solution.py:29
  367.1 8.0 %collective-permute-start.2 = (f32[1,96,256]{2,1,0:T(8,128)S(1)}, f32[1,96,256]{2,1,0:T(8,128)S(1)}, u32[]{:S(2)}, u32[]{:S(2)}) collective-permute-start(f32[1,96,256]{2,1,0:T(8,128)S(1)} %get-tuple-element.396), channel_id=1, source_target_pairs={{0,1},{1,2},{2,3},{3,4},{4,5},{5,6},{6,7},{7,8},{8,9},{9,10},{10,1... | collective-permute-start | bytes 294920 | tf_op jit(solution)/shard_map/while/body/eval_jaxpr/ppermute | solution.py:18
  378.1 8.0 %collective-permute-start.4 = (f32[1,96,256]{2,1,0:T(8,128)S(1)}, f32[1,96,256]{2,1,0:T(8,128)S(1)}, u32[]{:S(2)}, u32[]{:S(2)}) collective-permute-start(f32[1,96,256]{2,1,0:T(8,128)S(1)} %get-tuple-element.399), channel_id=1, source_target_pairs={{0,1},{1,2},{2,3},{3,4},{4,5},{5,6},{6,7},{7,8},{8,9},{9,10},{10,1... | collective-permute-start | bytes 294920 | tf_op jit(solution)/shard_map/while/body/eval_jaxpr/ppermute | solution.py:18
  401.5 8.4 %collective-permute-start.8 = (f32[1,96,256]{2,1,0:T(8,128)}, f32[1,96,256]{2,1,0:T(8,128)}, u32[]{:S(2)}, u32[]{:S(2)}) collective-permute-start(f32[1,96,256]{2,1,0:T(8,128)} %get-tuple-element.404), channel_id=1, source_target_pairs={{0,1},{1,2},{2,3},{3,4},{4,5},{5,6},{6,7},{7,8},{8,9},{9,10},{10,1... | collective-permute-start | bytes 294920 | tf_op jit(solution)/shard_map/while/body/eval_jaxpr/ppermute | solution.py:18
  413.6 12.4 %collective-permute-start = (f32[5,96,256]{2,1,0:T(8,128)}, f32[5,96,256]{2,1,0:T(8,128)S(1)}, u32[]{:S(2)}, u32[]{:S(2)}) collective-permute-start(f32[5,96,256]{2,1,0:T(8,128)} %bitcast.39), channel_id=1, source_target_pairs={{0,32},{32,64},{64,96},{96,128},{128,160},{160,192},{192,224},{1,3... | collective-permute-start | bytes 1474568 | tf_op jit(solution)/shard_map/while/body/eval_jaxpr/ppermute | solution.py:29
  429.2 8.0 %collective-permute-start.2 = (f32[1,96,256]{2,1,0:T(8,128)S(1)}, f32[1,96,256]{2,1,0:T(8,128)S(1)}, u32[]{:S(2)}, u32[]{:S(2)}) collective-permute-start(f32[1,96,256]{2,1,0:T(8,128)S(1)} %get-tuple-element.396), channel_id=1, source_target_pairs={{0,1},{1,2},{2,3},{3,4},{4,5},{5,6},{6,7},{7,8},{8,9},{9,10},{10,1... | collective-permute-start | bytes 294920 | tf_op jit(solution)/shard_map/while/body/eval_jaxpr/ppermute | solution.py:18
  463.6 8.4 %collective-permute-start.8 = (f32[1,96,256]{2,1,0:T(8,128)}, f32[1,96,256]{2,1,0:T(8,128)}, u32[]{:S(2)}, u32[]{:S(2)}) collective-permute-start(f32[1,96,256]{2,1,0:T(8,128)} %get-tuple-element.404), channel_id=1, source_target_pairs={{0,1},{1,2},{2,3},{3,4},{4,5},{5,6},{6,7},{7,8},{8,9},{9,10},{10,1... | collective-permute-start | bytes 294920 | tf_op jit(solution)/shard_map/while/body/eval_jaxpr/ppermute | solution.py:18
  475.7 12.4 %collective-permute-start = (f32[5,96,256]{2,1,0:T(8,128)}, f32[5,96,256]{2,1,0:T(8,128)S(1)}, u32[]{:S(2)}, u32[]{:S(2)}) collective-permute-start(f32[5,96,256]{2,1,0:T(8,128)} %bitcast.39), channel_id=1, source_target_pairs={{0,32},{32,64},{64,96},{96,128},{128,160},{160,192},{192,224},{1,3... | collective-permute-start | bytes 1474568 | tf_op jit(solution)/shard_map/while/body/eval_jaxpr/ppermute | solution.py:29
  513.4 8.0 %collective-permute-start.6 = (f32[1,96,256]{2,1,0:T(8,128)S(1)}, f32[1,96,256]{2,1,0:T(8,128)S(1)}, u32[]{:S(2)}, u32[]{:S(2)}) collective-permute-start(f32[1,96,256]{2,1,0:T(8,128)S(1)} %get-tuple-element.402), channel_id=1, source_target_pairs={{0,1},{1,2},{2,3},{3,4},{4,5},{5,6},{6,7},{7,8},{8,9},{9,10},{10,1... | collective-permute-start | bytes 294920 | tf_op jit(solution)/shard_map/while/body/eval_jaxpr/ppermute | solution.py:18
  525.8 8.4 %collective-permute-start.8 = (f32[1,96,256]{2,1,0:T(8,128)}, f32[1,96,256]{2,1,0:T(8,128)}, u32[]{:S(2)}, u32[]{:S(2)}) collective-permute-start(f32[1,96,256]{2,1,0:T(8,128)} %get-tuple-element.404), channel_id=1, source_target_pairs={{0,1},{1,2},{2,3},{3,4},{4,5},{5,6},{6,7},{7,8},{8,9},{9,10},{10,1... | collective-permute-start | bytes 294920 | tf_op jit(solution)/shard_map/while/body/eval_jaxpr/ppermute | solution.py:18
  537.8 12.4 %collective-permute-start = (f32[5,96,256]{2,1,0:T(8,128)}, f32[5,96,256]{2,1,0:T(8,128)S(1)}, u32[]{:S(2)}, u32[]{:S(2)}) collective-permute-start(f32[5,96,256]{2,1,0:T(8,128)} %bitcast.39), channel_id=1, source_target_pairs={{0,32},{32,64},{64,96},{96,128},{128,160},{160,192},{192,224},{1,3... | collective-permute-start | bytes 1474568 | tf_op jit(solution)/shard_map/while/body/eval_jaxpr/ppermute | solution.py:29
  587.9 8.4 %collective-permute-start.8 = (f32[1,96,256]{2,1,0:T(8,128)}, f32[1,96,256]{2,1,0:T(8,128)}, u32[]{:S(2)}, u32[]{:S(2)}) collective-permute-start(f32[1,96,256]{2,1,0:T(8,128)} %get-tuple-element.404), channel_id=1, source_target_pairs={{0,1},{1,2},{2,3},{3,4},{4,5},{5,6},{6,7},{7,8},{8,9},{9,10},{10,1... | collective-permute-start | bytes 294920 | tf_op jit(solution)/shard_map/while/body/eval_jaxpr/ppermute | solution.py:18
  599.9 12.4 %collective-permute-start = (f32[5,96,256]{2,1,0:T(8,128)}, f32[5,96,256]{2,1,0:T(8,128)S(1)}, u32[]{:S(2)}, u32[]{:S(2)}) collective-permute-start(f32[5,96,256]{2,1,0:T(8,128)} %bitcast.39), channel_id=1, source_target_pairs={{0,32},{32,64},{64,96},{96,128},{128,160},{160,192},{192,224},{1,3... | collective-permute-start | bytes 1474568 | tf_op jit(solution)/shard_map/while/body/eval_jaxpr/ppermute | solution.py:29
  615.6 8.0 %collective-permute-start.2 = (f32[1,96,256]{2,1,0:T(8,128)S(1)}, f32[1,96,256]{2,1,0:T(8,128)S(1)}, u32[]{:S(2)}, u32[]{:S(2)}) collective-permute-start(f32[1,96,256]{2,1,0:T(8,128)S(1)} %get-tuple-element.396), channel_id=1, source_target_pairs={{0,1},{1,2},{2,3},{3,4},{4,5},{5,6},{6,7},{7,8},{8,9},{9,10},{10,1... | collective-permute-start | bytes 294920 | tf_op jit(solution)/shard_map/while/body/eval_jaxpr/ppermute | solution.py:18
  650.0 8.4 %collective-permute-start.8 = (f32[1,96,256]{2,1,0:T(8,128)}, f32[1,96,256]{2,1,0:T(8,128)}, u32[]{:S(2)}, u32[]{:S(2)}) collective-permute-start(f32[1,96,256]{2,1,0:T(8,128)} %get-tuple-element.404), channel_id=1, source_target_pairs={{0,1},{1,2},{2,3},{3,4},{4,5},{5,6},{6,7},{7,8},{8,9},{9,10},{10,1... | collective-permute-start | bytes 294920 | tf_op jit(solution)/shard_map/while/body/eval_jaxpr/ppermute | solution.py:18
  662.1 12.4 %collective-permute-start = (f32[5,96,256]{2,1,0:T(8,128)}, f32[5,96,256]{2,1,0:T(8,128)S(1)}, u32[]{:S(2)}, u32[]{:S(2)}) collective-permute-start(f32[5,96,256]{2,1,0:T(8,128)} %bitcast.39), channel_id=1, source_target_pairs={{0,32},{32,64},{64,96},{96,128},{128,160},{160,192},{192,224},{1,3... | collective-permute-start | bytes 1474568 | tf_op jit(solution)/shard_map/while/body/eval_jaxpr/ppermute | solution.py:29
  699.7 8.0 %collective-permute-start.6 = (f32[1,96,256]{2,1,0:T(8,128)S(1)}, f32[1,96,256]{2,1,0:T(8,128)S(1)}, u32[]{:S(2)}, u32[]{:S(2)}) collective-permute-start(f32[1,96,256]{2,1,0:T(8,128)S(1)} %get-tuple-element.402), channel_id=1, source_target_pairs={{0,1},{1,2},{2,3},{3,4},{4,5},{5,6},{6,7},{7,8},{8,9},{9,10},{10,1... | collective-permute-start | bytes 294920 | tf_op jit(solution)/shard_map/while/body/eval_jaxpr/ppermute | solution.py:18
  712.1 8.4 %collective-permute-start.8 = (f32[1,96,256]{2,1,0:T(8,128)}, f32[1,96,256]{2,1,0:T(8,128)}, u32[]{:S(2)}, u32[]{:S(2)}) collective-permute-start(f32[1,96,256]{2,1,0:T(8,128)} %get-tuple-element.404), channel_id=1, source_target_pairs={{0,1},{1,2},{2,3},{3,4},{4,5},{5,6},{6,7},{7,8},{8,9},{9,10},{10,1... | collective-permute-start | bytes 294920 | tf_op jit(solution)/shard_map/while/body/eval_jaxpr/ppermute | solution.py:18
  (125 other events, 1050.8 us)
where the time goes:
time: 728 us; the launch traced here: 724 us
  starting transfers between devices  313 us (43%)
  waiting for transfers between devices  289 us (40%)
  other arithmetic  101 us (14%)
  local copies, waits for them, and re-layouts  16.5 us (2%)
    ppermute x52, waiting for transfers between devices, with_halo(): lax.ppermute(lax.slice_in_dim(block, block.shape[dim] - width, None, axis...  184 us
    ppermute x52, starting transfers between devices, with_halo(): lax.ppermute(lax.slice_in_dim(block, 0, width, axis=dim), axis, backward)  182 us
    ppermute x52, starting transfers between devices, with_halo(): lax.ppermute(lax.slice_in_dim(block, block.shape[dim] - width, None, axis...  115 us
    ppermute x8, waiting for transfers between devices, shifted(): return lax.ppermute(shard, axis, pairs)  82.8 us
    div x41, other arithmetic, implicit(): field = sweep_sum(rhs, faces, side_pad(up)) / diag  37.5 us
    concatenate x52, other arithmetic, with_halo(): block = jnp.concatenate([low, block, high], axis=dim)  28.5 us
    ppermute x52, waiting for transfers between devices, with_halo(): lax.ppermute(lax.slice_in_dim(block, 0, width, axis=dim), axis, backward)  22 us
    another operation x8, other arithmetic, one_round(): return jnp.stack(result)  17.9 us
  transfers between devices with their start and end apart: 112, of which 68 were waited for; matrix products, arithmetic and copies ran while one was open for 1% of the time, Pallas kernels for 0%

commit v1 on v0

v1 whole, which is shorter than its diff:
```python
import functools
import jax
import jax.numpy as jnp
from jax import lax
from jax.experimental import pallas as pl
from jax.experimental.pallas import tpu as pltpu
from jax.sharding import PartitionSpec as P

F32 = jnp.float32
VM = pl.BlockSpec(memory_space=pltpu.VMEM)
SM = pl.BlockSpec(memory_space=pltpu.SMEM)
NY, NZ = 96, 256
NL = 5
W = 4
EXT = NL + 2 * W
SLAB = 12
HR = 40
OWN = 16


def call(body, outs, ins, scratch=(), name=None, flops=0, limit=40):
    return pl.pallas_call(
        body,
        out_shape=[jax.ShapeDtypeStruct(s, F32) for s in outs],
        in_specs=ins,
        out_specs=[VM] * len(outs),
        scratch_shapes=list(scratch),
        compiler_params=pltpu.CompilerParams(vmem_limit_bytes=limit * 2**20),
        cost_estimate=pl.CostEstimate(flops=flops, bytes_accessed=4_000_000, transcendentals=0),
        name=name,
    )


def up_roll(x, axis):
    return pltpu.roll(x, x.shape[axis] - 1, axis)


def down_roll(x, axis):
    return pltpu.roll(x, 1, axis)


def sweep_layer(l, src, beta, fx, fy, fz, inv):
    w = src[l]
    a = fy[l]
    b = fz[l]
    total = beta[l] + fx[l] * src[l - 1] + fx[l + 1] * src[l + 1]
    total = total + a * down_roll(w, 0) + up_roll(a * w, 0)
    total = total + b * down_roll(w, 1) + up_roll(b * w, 1)
    return total * inv[l]


def sweeps(wa, wb, beta, fx, fy, fz, inv, finish):
    for n, (src, dst) in enumerate(((wa, wb), (wb, wa), (wa, wb))):
        def one(l, _):
            dst[l] = sweep_layer(l, src, beta, fx, fy, fz, inv)
            return 0
        lax.fori_loop(n + 1, EXT - 1 - n, one, 0)
    def last(l, _):
        finish(l, sweep_layer(l, wb, beta, fx, fy, fz, inv))
        return 0
    lax.fori_loop(W, W + NL, last, 0)


def place_halo(par, dst, on, off, first, count):
    @pl.when(par == 0)
    def _():
        dst[W - count:W] = off[first:first + count]
        dst[W + NL:W + NL + count] = on[first:first + count]

    @pl.when(par == 1)
    def _():
        dst[W - count:W] = on[first:first + count]
        dst[W + NL:W + NL + count] = off[first:first + count]


def give_edges(par, src, at, on, off, first, count):
    @pl.when(par == 0)
    def _():
        on[first:first + count] = src[at + NL - count:at + NL]
        off[first:first + count] = src[at:at + count]

    @pl.when(par == 1)
    def _():
        on[first:first + count] = src[at:at + count]
        off[first:first + count] = src[at + NL - count:at + NL]


def prep_body(ids, c, region, scale, source, cond, cap, on, off):
    par = ids[1] % 2
    r = region[...]
    cap[...] = jnp.where(r == 0, 2.0, jnp.where(r == 1, 1.2, 1.6)).astype(F32)
    cond[...] = jnp.where(r == 0, 0.3, jnp.where(r == 1, 4.0, 2.5)).astype(F32) * scale[...]
    give_edges(par, c, 0, on, off, 0, 4)
    give_edges(par, cond, 0, on, off, 4, 4)
    give_edges(par, cap, 0, on, off, 8, 3)
    give_edges(par, source, 0, on, off, 11, 3)


def first_body(ids, plan, c, cond, cap, source, on, off,
               u, fx, fy, fz, inv, capx, srcx, invc, son, soff,
               condx, wa, wb, beta):
    sp = ids[1]
    par = sp % 2
    condx[W:W + NL] = cond[...]
    capx[W:W + NL] = cap[...]
    srcx[W:W + NL] = source[...]
    wa[W:W + NL] = c[...]
    place_halo(par, wa, on, off, 0, 4)
    place_halo(par, condx, on, off, 4, 4)
    place_halo(par, capx, on, off, 8, 3)
    place_halo(par, srcx, on, off, 11, 3)
    zero = jnp.zeros((W, NY, NZ), F32)

    @pl.when(sp == 0)
    def _():
        condx[0:W] = zero

    @pl.when(sp == ids[2] - 1)
    def _():
        condx[W + NL:EXT] = zero

    rows = lax.broadcasted_iota(jnp.int32, (NY, NZ), 0)
    lanes = lax.broadcasted_iota(jnp.int32, (NY, NZ), 1)
    amp = plan[0].astype(F32) * 0.5

    def coef(l, _):
        k = condx[l]
        f0 = 0.5 * (k + condx[l - 1])
        f1 = 0.5 * (k + condx[l + 1])
        f2 = 0.5 * (k + jnp.where(rows == 0, 0.0, down_roll(k, 0)))
        f3 = 0.5 * (k + jnp.where(rows == NY - 1, 0.0, up_roll(k, 0)))
        f4 = 0.5 * (k + jnp.where(lanes == 0, 0.0, down_roll(k, 1)))
        f5 = 0.5 * (k + jnp.where(lanes == NZ - 1, 0.0, up_roll(k, 1)))
        total = ((((f0 + f1) + f2) + f3) + f4) + f5
        heat = capx[l]
        fx[l] = f0
        fy[l] = jnp.where(rows == 0, 0.0, f2)
        fz[l] = jnp.where(lanes == 0, 0.0, f4)
        inv[l] = 1.0 / (heat * 4.0 + total)
        invc[l] = 1.0 / (heat + total)
        beta[l] = heat * 4.0 * wa[l] + amp * srcx[l]
        return 0
    lax.fori_loop(1, EXT - 1, coef, 0)
    fx[EXT - 1] = 0.5 * (condx[EXT - 1] + condx[EXT - 2])

    @pl.when(sp == 0)
    def _():
        fx[W] = jnp.zeros((NY, NZ), F32)

    @pl.when(sp == ids[2] - 1)
    def _():
        fx[W + NL] = jnp.zeros((NY, NZ), F32)

    def finish(l, v):
        u[l - W] = v
    sweeps(wa, wb, beta, fx, fy, fz, inv, finish)
    give_edges(par, u, 0, son, soff, 0, 4)


def fine_body(j, ids, plan, u_old, fx, fy, fz, inv, capx, srcx, on, off, u, son, soff, wa, wb, beta):
    par = ids[1] % 2
    wa[W:W + NL] = u_old[...]
    place_halo(par, wa, on, off, 0, 4)
    amp = plan[j].astype(F32) * 0.5

    def rhs(l, _):
        beta[l] = capx[l] * 4.0 * wa[l] + amp * srcx[l]
        return 0
    lax.fori_loop(1, EXT - 1, rhs, 0)

    def finish(l, v):
        u[l - W] = v
    sweeps(wa, wb, beta, fx, fy, fz, inv, finish)
    give_edges(par, u, 0, son, soff, 0, 4)


def last_body(j, ids, plan, u_old, fx, fy, fz, inv, capx, srcx, on, off, c_next, u, give, wa, wb, beta):
    par = ids[1] % 2
    wa[W:W + NL] = u_old[...]
    place_halo(par, wa, on, off, 0, 4)
    amp = plan[j].astype(F32) * 0.5

    def rhs(l, _):
        beta[l] = capx[l] * 4.0 * wa[l] + amp * srcx[l]
        return 0
    lax.fori_loop(1, EXT - 1, rhs, 0)

    def finish(l, v):
        u[l - W] = v
    sweeps(wa, wb, beta, fx, fy, fz, inv, finish)
    for l in range(NL):
        d = u[l] - c_next[l]
        for t in range(8):
            part = d[t * SLAB:(t + 1) * SLAB]
            give[t, l * SLAB:(l + 1) * SLAB] = part[:, :128]
            give[t, 60 + l * SLAB:60 + (l + 1) * SLAB] = part[:, 128:]


def slab_body(ids, fx, fy, fz, invc, capx, out):
    shift = (16 + 128 - 12 * ids[0]) % 128
    spare = jnp.zeros((128 - NY, NZ), F32)
    for n, ref in enumerate((fx, fy, fz, invc, capx)):
        def one(l, _):
            v = jnp.concatenate([ref[l], spare], axis=0)
            out[n, l] = pltpu.roll(v, shift, 0)[:HR]
            return 0
        lax.fori_loop(1, EXT if n == 0 else EXT - 1, one, 0)


def unpack(chunk, l):
    return jnp.concatenate([chunk[l * SLAB:(l + 1) * SLAB], chunk[60 + l * SLAB:60 + (l + 1) * SLAB]], axis=1)


DEPTHS = ((1, 12, 0), (2, 8, 12), (3, 4, 20), (5, 4, 24), (7, 4, 28))


def ypay_body(got, fwd, bwd):
    for l in range(NL):
        for k, deep, at in DEPTHS:
            v = unpack(got[k - 1], l)
            fwd[l, at:at + deep] = v[SLAB - deep:]
            bwd[l, at:at + deep] = v[:deep]


def ymerge_body(ids, got, low, high, dx, on, off):
    dx[...] = jnp.zeros((7, NL, HR, NZ), F32)
    halo = {k: (deep, at) for k, deep, at in DEPTHS}
    for l in range(NL):
        for k in range(1, 8):
            dx[k - 1, l, OWN:OWN + SLAB] = unpack(got[k - 1], l)
            if k in halo:
                deep, at = halo[k]
                dx[k - 1, l, OWN - deep:OWN] = low[l, at:at + deep]
                dx[k - 1, l, OWN + SLAB:OWN + SLAB + deep] = high[l, at:at + deep]
    give_edges(ids[1] % 2, dx.at[0], 0, on, off, 0, 4)


def merge_body(ids, e, low, high, ex, on, off):
    ex[...] = e[...]
    ex[:, OWN - 8:OWN] = low[...]
    ex[:, OWN + SLAB:OWN + SLAB + 8] = high[...]
    give_edges(ids[1] % 2, ex, 0, on, off, 0, 4)


def stage_body(k, kind, ids, coef, e, on, off, *rest):
    par = ids[1] % 2
    if kind == "last":
        a, wa, wb, beta = rest
    else:
        dx, a, nxt, p, q, wa, wb, beta = rest
    wa[W:W + NL] = e[...]
    place_halo(par, wa, on, off, 0, 4)
    fx, fy, fz, inv, cap = (coef.at[n] for n in range(5))

    def rhs(l, _):
        beta[l] = cap[l] * wa[l]
        return 0
    lax.fori_loop(1, EXT - 1, rhs, 0)

    def finish(l, v):
        wa[l] = v
    sweeps(wa, wb, beta, fx, fy, fz, inv, finish)
    for l in range(NL):
        v = wa[W + l]
        part = v[OWN:OWN + SLAB]
        a[l * SLAB:(l + 1) * SLAB] = part[:, :128]
        a[60 + l * SLAB:60 + (l + 1) * SLAB] = part[:, 128:]
        if kind != "last":
            nxt[l] = v + dx[k, l]
    if kind == "x":
        give_edges(par, nxt, 0, p, q, 0, 4)
    if kind == "y":
        p[...] = nxt[:, OWN + SLAB - 8:OWN + SLAB]
        q[...] = nxt[:, OWN:OWN + 8]


def final_body(f, got, out):
    for l in range(NL):
        for t in range(8):
            out[l, t * SLAB:(t + 1) * SLAB] = f[l, t * SLAB:(t + 1) * SLAB] + unpack(got[t], l)


def swap_on(x):
    n = lax.axis_size("space")
    return lax.ppermute(x, "space", [(i, i ^ 1) for i in range(n)])


def swap_off(x):
    n = lax.axis_size("space")
    return lax.ppermute(x, "space", [(i, (i + 1) % n if i % 2 else (i - 1) % n) for i in range(n)])


def round_x(on, off):
    got_off = swap_off(off)
    return swap_on(on), got_off


def shift_tm(x, by):
    n = lax.axis_size("tm")
    return lax.ppermute(x, "tm", [(i, (i + by) % n) for i in range(n)])


def on_device(c_points, region, cond_scale, source, plan):
    c = c_points[0]
    ids = jnp.stack([lax.axis_index("tm"), lax.axis_index("space"), lax.axis_size("space")]).astype(jnp.int32)
    own, edge, ext = (NL, NY, NZ), (W, NY, NZ), (EXT, NY, NZ)
    work = [pltpu.VMEM(ext, F32)] * 3
    cond, cap, on, off = call(prep_body, [own, own, (14, NY, NZ), (14, NY, NZ)], [SM] + [VM] * 4, name="prep")(
        ids, c, region, cond_scale, source)
    on, off = round_x(on, off)
    c_next = shift_tm(c, -1)
    u, fx, fy, fz, inv, capx, srcx, invc, on, off = call(
        first_body, [own] + [ext] * 7 + [edge] * 2, [SM, SM] + [VM] * 6,
        [pltpu.VMEM(ext, F32)] * 4, name="fine0", flops=40_000_000)(ids, plan, c, cond, cap, source, on, off)
    (coef,) = call(slab_body, [(5, EXT, HR, NZ)], [SM] + [VM] * 5, name="slab")(ids, fx, fy, fz, invc, capx)
    fine = [u]
    for j in (1, 2):
        on, off = round_x(on, off)
        u, on, off = call(functools.partial(fine_body, j), [own, edge, edge], [SM, SM] + [VM] * 9, work,
                          name="fine", flops=30_000_000)(ids, plan, u, fx, fy, fz, inv, capx, srcx, on, off)
        fine.append(u)
    on, off = round_x(on, off)
    u, give = call(functools.partial(last_body, 3), [own, (8, 120, 128)], [SM, SM] + [VM] * 10, work,
                   name="fine3", flops=30_000_000)(ids, plan, u, fx, fy, fz, inv, capx, srcx, on, off, c_next)
    fine.append(u)
    got = lax.all_to_all(give, "tm", 0, 0, tiled=True)
    fwd, bwd = call(ypay_body, [(NL, 32, NZ)] * 2, [VM], name="ypay")(got)
    low, high = shift_tm(fwd, 1), shift_tm(bwd, -1)
    slab, side = (NL, HR, NZ), (W, HR, NZ)
    dx, on, off = call(ymerge_body, [(7,) + slab, side, side], [SM] + [VM] * 3, name="ymerge")(ids, got, low, high)
    e = dx[0]
    small = [pltpu.VMEM((EXT, HR, NZ), F32)] * 3
    parts = [jnp.zeros((120, 128), F32)]
    for k in range(1, 8):
        on, off = round_x(on, off)
        kind = "last" if k == 7 else "y" if k in (3, 5) else "x"
        body = functools.partial(stage_body, k, kind)
        if kind == "last":
            (a,) = call(body, [(120, 128)], [SM] + [VM] * 4, small, name="stage")(ids, coef, e, on, off)
        else:
            pay = (NL, 8, NZ) if kind == "y" else side
            a, e, p, q = call(body, [(120, 128), slab, pay, pay], [SM] + [VM] * 5, small, name="stage")(
                ids, coef, e, on, off, dx)
            if kind == "y":
                low, high = shift_tm(p, 1), shift_tm(q, -1)
                e, on, off = call(merge_body, [slab, side, side], [SM] + [VM] * 3, name="merge")(ids, e, low, high)
            else:
                on, off = p, q
        parts.append(a)
    back = lax.all_to_all(jnp.stack(parts), "tm", 0, 0, tiled=True)
    (corrected,) = call(final_body, [own], [VM] * 2, name="final")(u, back)
    return jnp.stack(fine), corrected[None]


def solution(mesh):
    in_specs = (
        P("tm", "space", None, None),
        P("space", None, None),
        P("space", None, None),
        P("space", None, None),
        P("tm"),
    )
    out_specs = (P("tm", "space", None, None), P("tm", "space", None, None))
    return jax.shard_map(
        on_device, mesh=mesh, in_specs=in_specs, out_specs=out_specs, check_vma=False
    )
```

time: 728 us -> 235 us (0.32)
  the two profiles are of different devices: /device:TPU:134 before, /device:TPU:32 now
where the time goes in v1:
time: 235 us; the launch traced here: 234 us
  waiting for transfers between devices  86.6 us (37%)
  starting transfers between devices  56.6 us (24%)
  local copies, waits for them, and re-layouts  37.1 us (16%)
  Pallas kernels  30.1 us (13%)
  blocking collectives  21.5 us (9%)
    ppermute x11, waiting for transfers between devices, swap_off(): lax.ppermute(x, 'space', [(i, (i + 1) % n if i % 2 else (i - 1) % n) for...  65.5 us
    ppermute x11, starting transfers between devices, swap_off(): lax.ppermute(x, 'space', [(i, (i + 1) % n if i % 2 else (i - 1) % n) for...  44.3 us
    pallas_call x6, local copies, waits for them, and re-layouts, on_device(): call(body, [(120, 128), slab, pay, pay], [SM] + [VM] * 5, small, name='st...  26.8 us
    all_to_all x1, blocking collectives, on_device(): got = lax.all_to_all(give, 'tm', 0, 0, tiled=True)  21.5 us
    all_to_all x1, waiting for transfers between devices, on_device(): back = lax.all_to_all(jnp.stack(parts), 'tm', 0, 0, tiled=True)  11.2 us
    pallas_call x2, Pallas kernels, on_device(): call(functools.partial(fine_body, j), [own, edge, edge], [SM, SM] + [VM]...  11 us
    ppermute x7, waiting for transfers between devices, shift_tm(): return lax.ppermute(x, 'tm', [(i, (i + by) % n) for i in range(n)])  9.79 us
    pallas_call x1, Pallas kernels, on_device(): call(first_body, [own] + [ext] * 7 + [edge] * 2, [SM, SM] + [VM] * 6, [pl...  8.09 us
  transfers between devices with their start and end apart: 30, of which 18 were waited for; matrix products, arithmetic and copies ran while one was open for 1% of the time, Pallas kernels for 3%

profile of v1, /device:TPU:32, one launch (start us, length us, event | category | flops | bytes accessed | tf_op | source)
XLA Modules:
  0.0 234.3 jit_solution(15104125427245299480)
XLA Ops:
  0.7 1.0 copy-done
  1.8 1.0 copy-done.2
  2.8 1.0 copy-done.4
  3.8 1.0 copy-done.5
  4.8 0.9 prep.1
  5.9 5.3 %collective-permute-start.1 = (f32[14,96,256]{2,1,0:T(8,128)S(1)}, f32[14,96,256]{2,1,0:T(8,128)S(1)}, u32[]{:S(2)}, u32[]{:S(2)}) collective-permute-start(f32[14,96,256]{2,1,0:T(8,128)S(1)} %get-tuple-element.62), channel_id=1, source_target_pairs={{0,31},{1,2},{2,1},{3,4},{4,3},{5,6},{6,5},{7,8},{8,7},{9,10},{10,... | collective-permute-start | bytes 4128776 | tf_op jit(solution)/shard_map/ppermute | solution.py:290
  11.2 16.0 %collective-permute-done.1.off = f32[14,96,256]{2,1,0:T(8,128)S(1)} collective-permute-done((f32[14,96,256]{2,1,0:T(8,128)S(1)}, f32[14,96,256]{2,1,0:T(8,128)S(1)}, u32[]{:S(2)}, u32[]{:S(2)}) %collective-permute-start.1) | collective-permute-done | bytes 1376288 | tf_op jit(solution)/shard_map/ppermute | solution.py:290
  27.2 1.1 copy-done.7
  28.2 8.1 %fine0.1 = (f32[5,96,256]{2,1,0:T(8,128)S(1)}, f32[13,96,256]{2,1,0:T(8,128)S(1)}, f32[13,96,256]{2,1,0:T(8,128)S(1)}, f32[13,96,256]{2,1,0:T(8,128)S(1)}, f32[1...) custom-call(s32[3]{0:T(128)S(1)} %pad_add_fusion.ids, ...), custom_call_target="tpu_custom_call" | custom-call | flops 40000000 | bytes 4000000 | tf_op jit(solution)/shard_map/fine0/pallas_call | solution.py:312
  36.4 5.1 %collective-permute-start.3 = (f32[4,96,256]{2,1,0:T(8,128)S(1)}, f32[4,96,256]{2,1,0:T(8,128)S(1)}, u32[]{:S(2)}, u32[]{:S(2)}) collective-permute-start(f32[4,96,256]{2,1,0:T(8,128)S(1)} %get-tuple-element.71), channel_id=1, source_target_pairs={{0,31},{1,2},{2,1},{3,4},{4,3},{5,6},{6,5},{7,8},{8,7},{9,10},{10,... | collective-permute-start | bytes 1179656 | tf_op jit(solution)/shard_map/ppermute | solution.py:290
  41.6 5.5 %collective-permute-done.3.off = f32[4,96,256]{2,1,0:T(8,128)S(1)} collective-permute-done((f32[4,96,256]{2,1,0:T(8,128)S(1)}, f32[4,96,256]{2,1,0:T(8,128)S(1)}, u32[]{:S(2)}, u32[]{:S(2)}) %collective-permute-start.3) | collective-permute-done | bytes 393248 | tf_op jit(solution)/shard_map/ppermute | solution.py:290
  47.1 5.5 %fine.2 = (f32[5,96,256]{2,1,0:T(8,128)S(1)}, f32[4,96,256]{2,1,0:T(8,128)S(1)}, f32[4,96,256]{2,1,0:T(8,128)S(1)}) custom-call(s32[3]{0:T(128)S(1)} %pad_add_fusion.ids, s32[4]{0:T(128)S(1)} %copy-done.6, f32[5,96,256]{2,1,0:T(8,128)S(1)} %get-tuple-element.63.u_old, f32[13,96,256]{2,1,0:T(8,128)S(1)} %get-tuple-element.64.fx, ...), custom_call_target="tpu_custom_call" | custom-call | flops 30000000 | bytes 4000000 | tf_op jit(solution)/shard_map/fine/pallas_call | solution.py:319
  52.6 0.1 collective-permute-start.4
  52.7 5.1 %collective-permute-start.5 = (f32[4,96,256]{2,1,0:T(8,128)S(1)}, f32[4,96,256]{2,1,0:T(8,128)S(1)}, u32[]{:S(2)}, u32[]{:S(2)}) collective-permute-start(f32[4,96,256]{2,1,0:T(8,128)S(1)} %get-tuple-element.74), channel_id=1, source_target_pairs={{0,31},{1,2},{2,1},{3,4},{4,3},{5,6},{6,5},{7,8},{8,7},{9,10},{10,... | collective-permute-start | bytes 1179656 | tf_op jit(solution)/shard_map/ppermute | solution.py:290
  57.8 0.1 collective-permute-start.8
  57.9 5.4 %collective-permute-done.5.off = f32[4,96,256]{2,1,0:T(8,128)S(1)} collective-permute-done((f32[4,96,256]{2,1,0:T(8,128)S(1)}, f32[4,96,256]{2,1,0:T(8,128)S(1)}, u32[]{:S(2)}, u32[]{:S(2)}) %collective-permute-start.5) | collective-permute-done | bytes 393248 | tf_op jit(solution)/shard_map/ppermute | solution.py:290
  63.3 5.5 %fine.3 = (f32[5,96,256]{2,1,0:T(8,128)S(1)}, f32[4,96,256]{2,1,0:T(8,128)S(1)}, f32[4,96,256]{2,1,0:T(8,128)S(1)}) custom-call(s32[3]{0:T(128)S(1)} %pad_add_fusion.ids, s32[4]{0:T(128)S(1)} %copy-done.6, f32[5,96,256]{2,1,0:T(8,128)S(1)} %get-tuple-element.72.u_old, f32[13,96,256]{2,1,0:T(8,128)S(1)} %get-tuple-element.64.fx, ...), custom_call_target="tpu_custom_call" | custom-call | flops 30000000 | bytes 4000000 | tf_op jit(solution)/shard_map/fine/pallas_call | solution.py:319
  68.8 0.1 collective-permute-start.6
  68.9 5.1 %collective-permute-start.7 = (f32[4,96,256]{2,1,0:T(8,128)S(1)}, f32[4,96,256]{2,1,0:T(8,128)S(1)}, u32[]{:S(2)}, u32[]{:S(2)}) collective-permute-start(f32[4,96,256]{2,1,0:T(8,128)S(1)} %get-tuple-element.77), channel_id=1, source_target_pairs={{0,31},{1,2},{2,1},{3,4},{4,3},{5,6},{6,5},{7,8},{8,7},{9,10},{10,... | collective-permute-start | bytes 1179656 | tf_op jit(solution)/shard_map/ppermute | solution.py:290
  74.0 5.5 %collective-permute-done.7.off = f32[4,96,256]{2,1,0:T(8,128)S(1)} collective-permute-done((f32[4,96,256]{2,1,0:T(8,128)S(1)}, f32[4,96,256]{2,1,0:T(8,128)S(1)}, u32[]{:S(2)}, u32[]{:S(2)}) %collective-permute-start.7) | collective-permute-done | bytes 393248 | tf_op jit(solution)/shard_map/ppermute | solution.py:290
  79.5 5.5 %fine3.1 = (f32[5,96,256]{2,1,0:T(8,128)S(1)}, f32[8,120,128]{2,1,0:T(8,128)S(1)}) custom-call(s32[3]{0:T(128)S(1)} %pad_add_fusion.ids, s32[4]{0:T(128)S(1)} %copy-done.6, f32[5,96,256]{2,1,0:T(8,128)S(1)} %get-tuple-element.75.u_old, f32[13,96,256]{2,1,0:T(8,128)S(1)} %get-tuple-element.64.fx, f32[13,96,256]{2,1,0:T(8,128)S(1)} %get-tuple-element.65.fy, ...), custom_call_target="tpu_custom_call" | custom-call | flops 30000000 | bytes 4000000 | tf_op jit(solution)/shard_map/fine3/pallas_call | solution.py:323
  85.0 21.5 %all_to_all.10.got = f32[8,120,128]{2,1,0:T(8,128)S(1)} all-to-all(f32[8,120,128]{2,1,0:T(8,128)S(1)} %get-tuple-element.80), channel_id=1, replica_groups=mesh['tm'=8,'space'=32] {'tm'}, dimensions={0} | all-to-all | bytes 983040 | tf_op jit(solution)/shard_map/all_to_all | solution.py:326
  106.6 1.4 collective-permute-start.10
  108.0 0.7 collective-permute-start.9
  108.7 0.6 broadcast_dynamic-update-slice_fusion
  109.3 1.8 slab.1
  111.1 0.9 collective-permute-done.10.high
  112.0 1.3 collective-permute-done.9.low
  113.3 0.7 ymerge.1
  114.1 4.5 %collective-permute-start.12 = (f32[4,40,256]{2,1,0:T(8,128)S(1)}, f32[4,40,256]{2,1,0:T(8,128)S(1)}, u32[]{:S(2)}, u32[]{:S(2)}) collective-permute-start(f32[4,40,256]{2,1,0:T(8,128)S(1)} %get-tuple-element.85), channel_id=1, source_target_pairs={{0,31},{1,2},{2,1},{3,4},{4,3},{5,6},{6,5},{7,8},{8,7},{9,10},{10,... | collective-permute-start | bytes 491528 | tf_op jit(solution)/shard_map/ppermute | solution.py:290
  118.7 3.8 %collective-permute-done.12 = f32[4,40,256]{2,1,0:T(8,128)S(1)} collective-permute-done((f32[4,40,256]{2,1,0:T(8,128)S(1)}, f32[4,40,256]{2,1,0:T(8,128)S(1)}, u32[]{:S(2)}, u32[]{:S(2)}) %collective-permute-start.12) | collective-permute-done | bytes 163872 | tf_op jit(solution)/shard_map/ppermute | solution.py:290
  122.5 4.5 %stage.13 = (f32[8,120,128]{2,1,0:T(8,128)}, f32[5,40,256]{2,1,0:T(8,128)S(1)}, f32[4,40,256]{2,1,0:T(8,128)S(1)}, f32[4,40,256]{2,1,0:T(8,128)S(1)}) fusion(f32[8,120,128]{2,1,0:T(8,128)} %broadcast_dynamic-update-slice_fusion, s32[3]{0:T(128)S(1)} %pad_add_fusion.ids, f32[5,13,40,256]{3,2,1,0:T(8,128)S(1)} %slab.1, ...), kind=kCustom, calls=%fused_computation.8 | custom fusion | bytes 5222412 | tf_op jit(solution)/shard_map/stage/pallas_call | solution.py:342
  126.9 4.3 %collective-permute-start.14 = (f32[4,40,256]{2,1,0:T(8,128)S(1)}, f32[4,40,256]{2,1,0:T(8,128)S(1)}, u32[]{:S(2)}, u32[]{:S(2)}) collective-permute-start(f32[4,40,256]{2,1,0:T(8,128)S(1)} %get-tuple-element.131), channel_id=1, source_target_pairs={{0,31},{1,2},{2,1},{3,4},{4,3},{5,6},{6,5},{7,8},{8,7},{9,10},{10,... | collective-permute-start | bytes 491528 | tf_op jit(solution)/shard_map/ppermute | solution.py:290
  131.2 3.8 %collective-permute-done.14 = f32[4,40,256]{2,1,0:T(8,128)S(1)} collective-permute-done((f32[4,40,256]{2,1,0:T(8,128)S(1)}, f32[4,40,256]{2,1,0:T(8,128)S(1)}, u32[]{:S(2)}, u32[]{:S(2)}) %collective-permute-start.14) | collective-permute-done | bytes 163872 | tf_op jit(solution)/shard_map/ppermute | solution.py:290
  135.0 4.5 %stage.12 = (f32[8,120,128]{2,1,0:T(8,128)}, f32[5,40,256]{2,1,0:T(8,128)S(1)}, f32[4,40,256]{2,1,0:T(8,128)S(1)}, f32[4,40,256]{2,1,0:T(8,128)S(1)}) fusion(f32[8,120,128]{2,1,0:T(8,128)} %get-tuple-element.126, s32[3]{0:T(128)S(1)} %pad_add_fusion.ids, f32[5,13,40,256]{3,2,1,0:T(8,128)S(1)} %slab.1, f32[5,40,256]{2,1,0:T(8,128)S(1)} %get-tuple-element.127, ...), kind=kCustom, calls=%fused_computation.7 | custom fusion | bytes 5222412 | tf_op jit(solution)/shard_map/stage/pallas_call | solution.py:342
  139.5 4.3 %collective-permute-start.16 = (f32[4,40,256]{2,1,0:T(8,128)S(1)}, f32[4,40,256]{2,1,0:T(8,128)S(1)}, u32[]{:S(2)}, u32[]{:S(2)}) collective-permute-start(f32[4,40,256]{2,1,0:T(8,128)S(1)} %get-tuple-element.123), channel_id=1, source_target_pairs={{0,31},{1,2},{2,1},{3,4},{4,3},{5,6},{6,5},{7,8},{8,7},{9,10},{10,... | collective-permute-start | bytes 491528 | tf_op jit(solution)/shard_map/ppermute | solution.py:290
  143.8 3.8 %collective-permute-done.16 = f32[4,40,256]{2,1,0:T(8,128)S(1)} collective-permute-done((f32[4,40,256]{2,1,0:T(8,128)S(1)}, f32[4,40,256]{2,1,0:T(8,128)S(1)}, u32[]{:S(2)}, u32[]{:S(2)}) %collective-permute-start.16) | collective-permute-done | bytes 163872 | tf_op jit(solution)/shard_map/ppermute | solution.py:290
  147.6 4.5 %stage.11 = (f32[8,120,128]{2,1,0:T(8,128)}, f32[5,40,256]{2,1,0:T(8,128)S(1)}, f32[5,8,256]{2,1,0:T(8,128)S(1)}, f32[5,8,256]{2,1,0:T(8,128)S(1)}) fusion(f32[8,120,128]{2,1,0:T(8,128)} %get-tuple-element.118, s32[3]{0:T(128)S(1)} %pad_add_fusion.ids, f32[5,13,40,256]{3,2,1,0:T(8,128)S(1)} %slab.1, f32[5,40,256]{2,1,0:T(8,128)S(1)} %get-tuple-element.119, ...), kind=kCustom, calls=%fused_computation.6 | custom fusion | bytes 4976652 | tf_op jit(solution)/shard_map/stage/pallas_call | solution.py:342
  152.0 0.7 collective-permute-start.17
  152.7 1.3 collective-permute-start.18
  154.0 2.0 collective-permute-done.17.low
  156.0 0.7 collective-permute-done.18.high
  156.7 0.6 merge.2
  157.4 2.8 %collective-permute-start.20 = (f32[4,40,256]{2,1,0:T(8,128)S(1)}, f32[4,40,256]{2,1,0:T(8,128)S(1)}, u32[]{:S(2)}, u32[]{:S(2)}) collective-permute-start(f32[4,40,256]{2,1,0:T(8,128)S(1)} %get-tuple-element.100), channel_id=1, source_target_pairs={{0,31},{1,2},{2,1},{3,4},{4,3},{5,6},{6,5},{7,8},{8,7},{9,10},{10,... | collective-permute-start | bytes 491528 | tf_op jit(solution)/shard_map/ppermute | solution.py:290
  160.2 5.4 %collective-permute-done.20 = f32[4,40,256]{2,1,0:T(8,128)S(1)} collective-permute-done((f32[4,40,256]{2,1,0:T(8,128)S(1)}, f32[4,40,256]{2,1,0:T(8,128)S(1)}, u32[]{:S(2)}, u32[]{:S(2)}) %collective-permute-start.20) | collective-permute-done | bytes 163872 | tf_op jit(solution)/shard_map/ppermute | solution.py:290
  165.5 4.5 %stage.10 = (f32[8,120,128]{2,1,0:T(8,128)}, f32[5,40,256]{2,1,0:T(8,128)S(1)}, f32[4,40,256]{2,1,0:T(8,128)S(1)}, f32[4,40,256]{2,1,0:T(8,128)S(1)}) fusion(f32[8,120,128]{2,1,0:T(8,128)} %get-tuple-element.134, s32[3]{0:T(128)S(1)} %pad_add_fusion.ids, f32[5,13,40,256]{3,2,1,0:T(8,128)S(1)} %slab.1, f32[5,40,256]{2,1,0:T(8,128)S(1)} %get-tuple-element.98, ...), kind=kCustom, calls=%fused_computation.5 | custom fusion | bytes 5222412 | tf_op jit(solution)/shard_map/stage/pallas_call | solution.py:342
  170.0 2.7 %collective-permute-start.22 = (f32[4,40,256]{2,1,0:T(8,128)S(1)}, f32[4,40,256]{2,1,0:T(8,128)S(1)}, u32[]{:S(2)}, u32[]{:S(2)}) collective-permute-start(f32[4,40,256]{2,1,0:T(8,128)S(1)} %get-tuple-element.163), channel_id=1, source_target_pairs={{0,31},{1,2},{2,1},{3,4},{4,3},{5,6},{6,5},{7,8},{8,7},{9,10},{10,... | collective-permute-start | bytes 491528 | tf_op jit(solution)/shard_map/ppermute | solution.py:290
  172.7 5.4 %collective-permute-done.22 = f32[4,40,256]{2,1,0:T(8,128)S(1)} collective-permute-done((f32[4,40,256]{2,1,0:T(8,128)S(1)}, f32[4,40,256]{2,1,0:T(8,128)S(1)}, u32[]{:S(2)}, u32[]{:S(2)}) %collective-permute-start.22) | collective-permute-done | bytes 163872 | tf_op jit(solution)/shard_map/ppermute | solution.py:290
  178.1 4.5 %stage.9 = (f32[8,120,128]{2,1,0:T(8,128)}, f32[5,40,256]{2,1,0:T(8,128)S(1)}, f32[5,8,256]{2,1,0:T(8,128)S(1)}, f32[5,8,256]{2,1,0:T(8,128)S(1)}) fusion(f32[8,120,128]{2,1,0:T(8,128)} %get-tuple-element.158, s32[3]{0:T(128)S(1)} %pad_add_fusion.ids, f32[5,13,40,256]{3,2,1,0:T(8,128)S(1)} %slab.1, f32[5,40,256]{2,1,0:T(8,128)S(1)} %get-tuple-element.159, ...), kind=kCustom, calls=%fused_computation.4 | custom fusion | bytes 4976652 | tf_op jit(solution)/shard_map/stage/pallas_call | solution.py:342
  182.6 1.7 collective-permute-start.23
  184.3 0.3 collective-permute-start.24
  184.6 2.0 collective-permute-done.23.low
  186.6 2.9 %collective-permute-done.24.high = f32[5,8,256]{2,1,0:T(8,128)S(1)} collective-permute-done((f32[5,8,256]{2,1,0:T(8,128)S(1)}, f32[5,8,256]{2,1,0:T(8,128)S(1)}, u32[]{:S(2)}, u32[]{:S(2)}) %collective-permute-start.24) | collective-permute-done | bytes 40992 | tf_op jit(solution)/shard_map/ppermute | solution.py:300
  189.5 0.6 merge.3
  190.2 2.5 %collective-permute-start.26 = (f32[4,40,256]{2,1,0:T(8,128)S(1)}, f32[4,40,256]{2,1,0:T(8,128)S(1)}, u32[]{:S(2)}, u32[]{:S(2)}) collective-permute-start(f32[4,40,256]{2,1,0:T(8,128)S(1)} %get-tuple-element.111), channel_id=1, source_target_pairs={{0,31},{1,2},{2,1},{3,4},{4,3},{5,6},{6,5},{7,8},{8,7},{9,10},{10,... | collective-permute-start | bytes 491528 | tf_op jit(solution)/shard_map/ppermute | solution.py:290
  192.7 5.6 %collective-permute-done.26 = f32[4,40,256]{2,1,0:T(8,128)S(1)} collective-permute-done((f32[4,40,256]{2,1,0:T(8,128)S(1)}, f32[4,40,256]{2,1,0:T(8,128)S(1)}, u32[]{:S(2)}, u32[]{:S(2)}) %collective-permute-start.26) | collective-permute-done | bytes 163872 | tf_op jit(solution)/shard_map/ppermute | solution.py:290
  198.3 4.5 %stage.8 = (f32[8,120,128]{2,1,0:T(8,128)}, f32[5,40,256]{2,1,0:T(8,128)S(1)}, f32[4,40,256]{2,1,0:T(8,128)S(1)}, f32[4,40,256]{2,1,0:T(8,128)S(1)}) fusion(f32[8,120,128]{2,1,0:T(8,128)} %get-tuple-element.150, s32[3]{0:T(128)S(1)} %pad_add_fusion.ids, f32[5,13,40,256]{3,2,1,0:T(8,128)S(1)} %slab.1, f32[5,40,256]{2,1,0:T(8,128)S(1)} %get-tuple-element.109, ...), kind=kCustom, calls=%fused_computation.3 | custom fusion | bytes 5222412 | tf_op jit(solution)/shard_map/stage/pallas_call | solution.py:342
  202.8 2.5 %collective-permute-start.28 = (f32[4,40,256]{2,1,0:T(8,128)S(1)}, f32[4,40,256]{2,1,0:T(8,128)S(1)}, u32[]{:S(2)}, u32[]{:S(2)}) collective-permute-start(f32[4,40,256]{2,1,0:T(8,128)S(1)} %get-tuple-element.147), channel_id=1, source_target_pairs={{0,31},{1,2},{2,1},{3,4},{4,3},{5,6},{6,5},{7,8},{8,7},{9,10},{10,... | collective-permute-start | bytes 491528 | tf_op jit(solution)/shard_map/ppermute | solution.py:290
  205.3 5.6 %collective-permute-done.28 = f32[4,40,256]{2,1,0:T(8,128)S(1)} collective-permute-done((f32[4,40,256]{2,1,0:T(8,128)S(1)}, f32[4,40,256]{2,1,0:T(8,128)S(1)}, u32[]{:S(2)}, u32[]{:S(2)}) %collective-permute-start.28) | collective-permute-done | bytes 163872 | tf_op jit(solution)/shard_map/ppermute | solution.py:290
  210.9 4.4 %stage.7 = f32[8,120,128]{2,1,0:T(8,128)} fusion(f32[8,120,128]{2,1,0:T(8,128)} %get-tuple-element.142, s32[3]{0:T(128)S(1)} %pad_add_fusion.ids, f32[5,13,40,256]{3,2,1,0:T(8,128)S(1)} %slab.1, f32[5,40,256]{2,1,0:T(8,128)S(1)} %get-tuple-element.143, f32[4,40,256]{2,1,0:T(8,128)S(1)} %collective-permute-done.27, f32[4,40,256]{2,1,0:T(8,128)S(1)} %collective-permute-done.28), kind=kCustom, calls=%fused_computation.2 | custom fusion | bytes 3256332 | tf_op jit(solution)/shard_map/stage/pallas_call | solution.py:339
  215.3 5.4 %all-to-all-start.1 = ((f32[8,120,128]{2,1,0:T(8,128)}), f32[8,120,128]{2,1,0:T(8,128)S(1)}, u32[]{:S(2)}, u32[]{:S(2)}) async-start(f32[8,120,128]{2,1,0:T(8,128)} %stage.7), calls=%async_computation.1 | async-start | bytes 983040 | tf_op jit(solution)/shard_map/all_to_all | solution.py:350
  220.7 1.4 pad_maximum_fusion
  222.2 11.2 %all-to-all-done.1.got = f32[8,120,128]{2,1,0:T(8,128)S(1)} async-done(((f32[8,120,128]{2,1,0:T(8,128)}), f32[8,120,128]{2,1,0:T(8,128)S(1)}, u32[]{:S(2)}, u32[]{:S(2)}) %all-to-all-start.1) | async-done | bytes 491552 | tf_op jit(solution)/shard_map/all_to_all | solution.py:350
  233.4 0.8 final.1
  (35 shorter events, 0.7 us)
Async XLA Ops:
  0.6 27.6 %copy-start.6 = (s32[4]{0:T(128)S(1)}, s32[4]{0:T(128)}, u32[]{:S(2)}) copy-start(s32[4]{0:T(128)} %plan.7) | copy-start | bytes 52
  0.7 1.0 copy-start
  1.8 1.0 copy-start.2
  2.8 1.0 copy-start.4
  3.8 1.0 copy-start.5
  4.8 23.4 %copy-start.1 = (f32[5,96,256]{2,1,0:T(8,128)S(1)}, f32[5,96,256]{2,1,0:T(8,128)}, u32[]{:S(2)}) copy-start(f32[5,96,256]{2,1,0:T(8,128)} %source.3) | copy-start | bytes 1474564
  5.8 5.4 %collective-permute-start = (f32[14,96,256]{2,1,0:T(8,128)S(1)}, f32[14,96,256]{2,1,0:T(8,128)S(1)}, u32[]{:S(2)}, u32[]{:S(2)}) collective-permute-start(f32[14,96,256]{2,1,0:T(8,128)S(1)} %get-tuple-element.61), channel_id=1, source_target_pairs={{0,1},{1,0},{2,3},{3,2},{4,5},{5,4},{6,7},{7,6},{8,9},{9,8},{10,11... | collective-permute-start | bytes 4128776 | tf_op jit(solution)/shard_map/ppermute | solution.py:285
  5.9 21.3 %collective-permute-start.1 = (f32[14,96,256]{2,1,0:T(8,128)S(1)}, f32[14,96,256]{2,1,0:T(8,128)S(1)}, u32[]{:S(2)}, u32[]{:S(2)}) collective-permute-start(f32[14,96,256]{2,1,0:T(8,128)S(1)} %get-tuple-element.62), channel_id=1, source_target_pairs={{0,31},{1,2},{2,1},{3,4},{4,3},{5,6},{6,5},{7,8},{8,7},{9,10},{10,... | collective-permute-start | bytes 4128776 | tf_op jit(solution)/shard_map/ppermute | solution.py:290
  27.2 1.1 copy-start.7
  36.3 5.2 %collective-permute-start.2 = (f32[4,96,256]{2,1,0:T(8,128)S(1)}, f32[4,96,256]{2,1,0:T(8,128)S(1)}, u32[]{:S(2)}, u32[]{:S(2)}) collective-permute-start(f32[4,96,256]{2,1,0:T(8,128)S(1)} %get-tuple-element.70), channel_id=1, source_target_pairs={{0,1},{1,0},{2,3},{3,2},{4,5},{5,4},{6,7},{7,6},{8,9},{9,8},{10,11... | collective-permute-start | bytes 1179656 | tf_op jit(solution)/shard_map/ppermute | solution.py:285
  36.4 10.6 %collective-permute-start.3 = (f32[4,96,256]{2,1,0:T(8,128)S(1)}, f32[4,96,256]{2,1,0:T(8,128)S(1)}, u32[]{:S(2)}, u32[]{:S(2)}) collective-permute-start(f32[4,96,256]{2,1,0:T(8,128)S(1)} %get-tuple-element.71), channel_id=1, source_target_pairs={{0,31},{1,2},{2,1},{3,4},{4,3},{5,6},{6,5},{7,8},{8,7},{9,10},{10,... | collective-permute-start | bytes 1179656 | tf_op jit(solution)/shard_map/ppermute | solution.py:290
  47.0 10.8 %copy-start.3 = (f32[1,5,96,256]{3,2,1,0:T(8,128)S(1)}, f32[1,5,96,256]{3,2,1,0:T(8,128)}, u32[]{:S(2)}) copy-start(f32[1,5,96,256]{3,2,1,0:T(8,128)} %param.5) | copy-start | bytes 1474564
  52.6 5.3 %collective-permute-start.4 = (f32[4,96,256]{2,1,0:T(8,128)S(1)}, f32[4,96,256]{2,1,0:T(8,128)S(1)}, u32[]{:S(2)}, u32[]{:S(2)}) collective-permute-start(f32[4,96,256]{2,1,0:T(8,128)S(1)} %get-tuple-element.73), channel_id=1, source_target_pairs={{0,1},{1,0},{2,3},{3,2},{4,5},{5,4},{6,7},{7,6},{8,9},{9,8},{10,11... | collective-permute-start | bytes 1179656 | tf_op jit(solution)/shard_map/ppermute | solution.py:285
  52.7 10.6 %collective-permute-start.5 = (f32[4,96,256]{2,1,0:T(8,128)S(1)}, f32[4,96,256]{2,1,0:T(8,128)S(1)}, u32[]{:S(2)}, u32[]{:S(2)}) collective-permute-start(f32[4,96,256]{2,1,0:T(8,128)S(1)} %get-tuple-element.74), channel_id=1, source_target_pairs={{0,31},{1,2},{2,1},{3,4},{4,3},{5,6},{6,5},{7,8},{8,7},{9,10},{10,... | collective-permute-start | bytes 1179656 | tf_op jit(solution)/shard_map/ppermute | solution.py:290
  57.8 16.2 %collective-permute-start.8 = (f32[5,96,256]{2,1,0:T(8,128)S(1)}, f32[5,96,256]{2,1,0:T(8,128)S(1)}, u32[]{:S(2)}, u32[]{:S(2)}) collective-permute-start(f32[5,96,256]{2,1,0:T(8,128)S(1)} %bitcast.26), channel_id=1, source_target_pairs={{0,224},{32,0},{64,32},{96,64},{128,96},{160,128},{192,160},{224,1... | collective-permute-start | bytes 1474568 | tf_op jit(solution)/shard_map/ppermute | solution.py:300
  68.8 5.2 %collective-permute-start.6 = (f32[4,96,256]{2,1,0:T(8,128)S(1)}, f32[4,96,256]{2,1,0:T(8,128)S(1)}, u32[]{:S(2)}, u32[]{:S(2)}) collective-permute-start(f32[4,96,256]{2,1,0:T(8,128)S(1)} %get-tuple-element.76), channel_id=1, source_target_pairs={{0,1},{1,0},{2,3},{3,2},{4,5},{5,4},{6,7},{7,6},{8,9},{9,8},{10,11... | collective-permute-start | bytes 1179656 | tf_op jit(solution)/shard_map/ppermute | solution.py:285
  68.9 10.6 %collective-permute-start.7 = (f32[4,96,256]{2,1,0:T(8,128)S(1)}, f32[4,96,256]{2,1,0:T(8,128)S(1)}, u32[]{:S(2)}, u32[]{:S(2)}) collective-permute-start(f32[4,96,256]{2,1,0:T(8,128)S(1)} %get-tuple-element.77), channel_id=1, source_target_pairs={{0,31},{1,2},{2,1},{3,4},{4,3},{5,6},{6,5},{7,8},{8,7},{9,10},{10,... | collective-permute-start | bytes 1179656 | tf_op jit(solution)/shard_map/ppermute | solution.py:290
  106.6 5.4 %collective-permute-start.10 = (f32[5,32,256]{2,1,0:T(8,128)S(1)}, f32[5,32,256]{2,1,0:T(8,128)S(1)}, u32[]{:S(2)}, u32[]{:S(2)}) collective-permute-start(f32[5,32,256]{2,1,0:T(8,128)S(1)} %get-tuple-element.82), channel_id=1, source_target_pairs={{0,224},{32,0},{64,32},{96,64},{128,96},{160,128},{192,160},{224,1... | collective-permute-start | bytes 491528 | tf_op jit(solution)/shard_map/ppermute | solution.py:300
  108.0 5.3 %collective-permute-start.9 = (f32[5,32,256]{2,1,0:T(8,128)S(1)}, f32[5,32,256]{2,1,0:T(8,128)S(1)}, u32[]{:S(2)}, u32[]{:S(2)}) collective-permute-start(f32[5,32,256]{2,1,0:T(8,128)S(1)} %get-tuple-element.81), channel_id=1, source_target_pairs={{0,32},{32,64},{64,96},{96,128},{128,160},{160,192},{192,224},{224... | collective-permute-start | bytes 491528 | tf_op jit(solution)/shard_map/ppermute | solution.py:300
  114.0 4.7 %collective-permute-start.11 = (f32[4,40,256]{2,1,0:T(8,128)S(1)}, f32[4,40,256]{2,1,0:T(8,128)S(1)}, u32[]{:S(2)}, u32[]{:S(2)}) collective-permute-start(f32[4,40,256]{2,1,0:T(8,128)S(1)} %get-tuple-element.84), channel_id=1, source_target_pairs={{0,1},{1,0},{2,3},{3,2},{4,5},{5,4},{6,7},{7,6},{8,9},{9,8},{10,11... | collective-permute-start | bytes 491528 | tf_op jit(solution)/shard_map/ppermute | solution.py:285
  114.1 8.3 %collective-permute-start.12 = (f32[4,40,256]{2,1,0:T(8,128)S(1)}, f32[4,40,256]{2,1,0:T(8,128)S(1)}, u32[]{:S(2)}, u32[]{:S(2)}) collective-permute-start(f32[4,40,256]{2,1,0:T(8,128)S(1)} %get-tuple-element.85), channel_id=1, source_target_pairs={{0,31},{1,2},{2,1},{3,4},{4,3},{5,6},{6,5},{7,8},{8,7},{9,10},{10,... | collective-permute-start | bytes 491528 | tf_op jit(solution)/shard_map/ppermute | solution.py:290
  126.9 4.3 %collective-permute-start.13 = (f32[4,40,256]{2,1,0:T(8,128)S(1)}, f32[4,40,256]{2,1,0:T(8,128)S(1)}, u32[]{:S(2)}, u32[]{:S(2)}) collective-permute-start(f32[4,40,256]{2,1,0:T(8,128)S(1)} %get-tuple-element.129), channel_id=1, source_target_pairs={{0,1},{1,0},{2,3},{3,2},{4,5},{5,4},{6,7},{7,6},{8,9},{9,8},{10,11... | collective-permute-start | bytes 491528 | tf_op jit(solution)/shard_map/ppermute | solution.py:285
  126.9 8.1 %collective-permute-start.14 = (f32[4,40,256]{2,1,0:T(8,128)S(1)}, f32[4,40,256]{2,1,0:T(8,128)S(1)}, u32[]{:S(2)}, u32[]{:S(2)}) collective-permute-start(f32[4,40,256]{2,1,0:T(8,128)S(1)} %get-tuple-element.131), channel_id=1, source_target_pairs={{0,31},{1,2},{2,1},{3,4},{4,3},{5,6},{6,5},{7,8},{8,7},{9,10},{10,... | collective-permute-start | bytes 491528 | tf_op jit(solution)/shard_map/ppermute | solution.py:290
  139.5 4.3 %collective-permute-start.15 = (f32[4,40,256]{2,1,0:T(8,128)S(1)}, f32[4,40,256]{2,1,0:T(8,128)S(1)}, u32[]{:S(2)}, u32[]{:S(2)}) collective-permute-start(f32[4,40,256]{2,1,0:T(8,128)S(1)} %get-tuple-element.121), channel_id=1, source_target_pairs={{0,1},{1,0},{2,3},{3,2},{4,5},{5,4},{6,7},{7,6},{8,9},{9,8},{10,11... | collective-permute-start | bytes 491528 | tf_op jit(solution)/shard_map/ppermute | solution.py:285
  139.5 8.1 %collective-permute-start.16 = (f32[4,40,256]{2,1,0:T(8,128)S(1)}, f32[4,40,256]{2,1,0:T(8,128)S(1)}, u32[]{:S(2)}, u32[]{:S(2)}) collective-permute-start(f32[4,40,256]{2,1,0:T(8,128)S(1)} %get-tuple-element.123), channel_id=1, source_target_pairs={{0,31},{1,2},{2,1},{3,4},{4,3},{5,6},{6,5},{7,8},{8,7},{9,10},{10,... | collective-permute-start | bytes 491528 | tf_op jit(solution)/shard_map/ppermute | solution.py:290
  152.0 4.0 %collective-permute-start.17 = (f32[5,8,256]{2,1,0:T(8,128)S(1)}, f32[5,8,256]{2,1,0:T(8,128)S(1)}, u32[]{:S(2)}, u32[]{:S(2)}) collective-permute-start(f32[5,8,256]{2,1,0:T(8,128)S(1)} %get-tuple-element.137), channel_id=1, source_target_pairs={{0,32},{32,64},{64,96},{96,128},{128,160},{160,192},{192,224},{224... | collective-permute-start | bytes 122888 | tf_op jit(solution)/shard_map/ppermute | solution.py:300
  152.7 4.0 %collective-permute-start.18 = (f32[5,8,256]{2,1,0:T(8,128)S(1)}, f32[5,8,256]{2,1,0:T(8,128)S(1)}, u32[]{:S(2)}, u32[]{:S(2)}) collective-permute-start(f32[5,8,256]{2,1,0:T(8,128)S(1)} %get-tuple-element.139), channel_id=1, source_target_pairs={{0,224},{32,0},{64,32},{96,64},{128,96},{160,128},{192,160},{224,1... | collective-permute-start | bytes 122888 | tf_op jit(solution)/shard_map/ppermute | solution.py:300
  157.3 2.9 %collective-permute-start.19 = (f32[4,40,256]{2,1,0:T(8,128)S(1)}, f32[4,40,256]{2,1,0:T(8,128)S(1)}, u32[]{:S(2)}, u32[]{:S(2)}) collective-permute-start(f32[4,40,256]{2,1,0:T(8,128)S(1)} %get-tuple-element.99), channel_id=1, source_target_pairs={{0,1},{1,0},{2,3},{3,2},{4,5},{5,4},{6,7},{7,6},{8,9},{9,8},{10,11... | collective-permute-start | bytes 491528 | tf_op jit(solution)/shard_map/ppermute | solution.py:285
  157.4 8.2 %collective-permute-start.20 = (f32[4,40,256]{2,1,0:T(8,128)S(1)}, f32[4,40,256]{2,1,0:T(8,128)S(1)}, u32[]{:S(2)}, u32[]{:S(2)}) collective-permute-start(f32[4,40,256]{2,1,0:T(8,128)S(1)} %get-tuple-element.100), channel_id=1, source_target_pairs={{0,31},{1,2},{2,1},{3,4},{4,3},{5,6},{6,5},{7,8},{8,7},{9,10},{10,... | collective-permute-start | bytes 491528 | tf_op jit(solution)/shard_map/ppermute | solution.py:290
  170.0 2.7 %collective-permute-start.21 = (f32[4,40,256]{2,1,0:T(8,128)S(1)}, f32[4,40,256]{2,1,0:T(8,128)S(1)}, u32[]{:S(2)}, u32[]{:S(2)}) collective-permute-start(f32[4,40,256]{2,1,0:T(8,128)S(1)} %get-tuple-element.161), channel_id=1, source_target_pairs={{0,1},{1,0},{2,3},{3,2},{4,5},{5,4},{6,7},{7,6},{8,9},{9,8},{10,11... | collective-permute-start | bytes 491528 | tf_op jit(solution)/shard_map/ppermute | solution.py:285
  170.0 8.1 %collective-permute-start.22 = (f32[4,40,256]{2,1,0:T(8,128)S(1)}, f32[4,40,256]{2,1,0:T(8,128)S(1)}, u32[]{:S(2)}, u32[]{:S(2)}) collective-permute-start(f32[4,40,256]{2,1,0:T(8,128)S(1)} %get-tuple-element.163), channel_id=1, source_target_pairs={{0,31},{1,2},{2,1},{3,4},{4,3},{5,6},{6,5},{7,8},{8,7},{9,10},{10,... | collective-permute-start | bytes 491528 | tf_op jit(solution)/shard_map/ppermute | solution.py:290
  182.6 4.0 %collective-permute-start.23 = (f32[5,8,256]{2,1,0:T(8,128)S(1)}, f32[5,8,256]{2,1,0:T(8,128)S(1)}, u32[]{:S(2)}, u32[]{:S(2)}) collective-permute-start(f32[5,8,256]{2,1,0:T(8,128)S(1)} %get-tuple-element.153), channel_id=1, source_target_pairs={{0,32},{32,64},{64,96},{96,128},{128,160},{160,192},{192,224},{224... | collective-permute-start | bytes 122888 | tf_op jit(solution)/shard_map/ppermute | solution.py:300
  184.3 5.2 %collective-permute-start.24 = (f32[5,8,256]{2,1,0:T(8,128)S(1)}, f32[5,8,256]{2,1,0:T(8,128)S(1)}, u32[]{:S(2)}, u32[]{:S(2)}) collective-permute-start(f32[5,8,256]{2,1,0:T(8,128)S(1)} %get-tuple-element.155), channel_id=1, source_target_pairs={{0,224},{32,0},{64,32},{96,64},{128,96},{160,128},{192,160},{224,1... | collective-permute-start | bytes 122888 | tf_op jit(solution)/shard_map/ppermute | solution.py:300
  190.1 2.7 %collective-permute-start.25 = (f32[4,40,256]{2,1,0:T(8,128)S(1)}, f32[4,40,256]{2,1,0:T(8,128)S(1)}, u32[]{:S(2)}, u32[]{:S(2)}) collective-permute-start(f32[4,40,256]{2,1,0:T(8,128)S(1)} %get-tuple-element.110), channel_id=1, source_target_pairs={{0,1},{1,0},{2,3},{3,2},{4,5},{5,4},{6,7},{7,6},{8,9},{9,8},{10,11... | collective-permute-start | bytes 491528 | tf_op jit(solution)/shard_map/ppermute | solution.py:285
  190.2 8.2 %collective-permute-start.26 = (f32[4,40,256]{2,1,0:T(8,128)S(1)}, f32[4,40,256]{2,1,0:T(8,128)S(1)}, u32[]{:S(2)}, u32[]{:S(2)}) collective-permute-start(f32[4,40,256]{2,1,0:T(8,128)S(1)} %get-tuple-element.111), channel_id=1, source_target_pairs={{0,31},{1,2},{2,1},{3,4},{4,3},{5,6},{6,5},{7,8},{8,7},{9,10},{10,... | collective-permute-start | bytes 491528 | tf_op jit(solution)/shard_map/ppermute | solution.py:290
  202.8 2.5 %collective-permute-start.27 = (f32[4,40,256]{2,1,0:T(8,128)S(1)}, f32[4,40,256]{2,1,0:T(8,128)S(1)}, u32[]{:S(2)}, u32[]{:S(2)}) collective-permute-start(f32[4,40,256]{2,1,0:T(8,128)S(1)} %get-tuple-element.145), channel_id=1, source_target_pairs={{0,1},{1,0},{2,3},{3,2},{4,5},{5,4},{6,7},{7,6},{8,9},{9,8},{10,11... | collective-permute-start | bytes 491528 | tf_op jit(solution)/shard_map/ppermute | solution.py:285
  202.8 8.1 %collective-permute-start.28 = (f32[4,40,256]{2,1,0:T(8,128)S(1)}, f32[4,40,256]{2,1,0:T(8,128)S(1)}, u32[]{:S(2)}, u32[]{:S(2)}) collective-permute-start(f32[4,40,256]{2,1,0:T(8,128)S(1)} %get-tuple-element.147), channel_id=1, source_target_pairs={{0,31},{1,2},{2,1},{3,4},{4,3},{5,6},{6,5},{7,8},{8,7},{9,10},{10,... | collective-permute-start | bytes 491528 | tf_op jit(solution)/shard_map/ppermute | solution.py:290
  215.3 18.1 %all-to-all-start.1 = ((f32[8,120,128]{2,1,0:T(8,128)}), f32[8,120,128]{2,1,0:T(8,128)S(1)}, u32[]{:S(2)}, u32[]{:S(2)}) async-start(f32[8,120,128]{2,1,0:T(8,128)} %stage.7), calls=%async_computation.1 | async-start | bytes 983040 | tf_op jit(solution)/shard_map/all_to_all | solution.py:350
